TPU v7x, 32 devices: a whole 2x2x4 slice. The times are simulated.
32 devices in a mesh: lat: 8 (over y, x, core), wave: 4 (over z).
Axes of the slice: x: 2, y: 2, z: 4, core: 2. Of those that a mesh axis runs over, the one named last changes fastest.
Arguments:
- fourier_rows: bfloat16 [128, 1600, 384], P('wave', 'lat'), may hold values from -0.796875 to 0.796875
- legendre: float32 [128, 1600, 800], P('wave', 'lat'), may hold values from -0.21875 to 0.21875
- wavenumber: int32 [128], replicated, may hold values from 0 to 1599, as said below
- lower_diag: float32 [128, 1600], P('wave'), may hold values from -0.9 to 0.9
- main_diag: float32 [128, 1600], P('wave'), may hold values from 2 to 4
- upper_diag: float32 [128, 1600], P('wave'), may hold values from -0.9 to 0.9
Outputs:
- grid: bfloat16 [3200, 307200], P('wave', 'lat')
Inputs may be any that keep to these rules, and one draw needn't show every extreme that they name: `wavenumber`: distinct wavenumbers; slot 2 i holds some a below 800 and slot 2 i + 1 holds 1599 - a; both ends of the range occur.
All inputs are finite; a program needn't handle non-finite values.
Results may differ from a plain program's by a relative error of at most 0.0055.
Values may be sent and summed in bfloat16 or wider, within the bound.
No kernel may reach another device: no remote copies, remote signals or barrier semaphores. Data moves between devices by JAX's collectives and lax.ppermute only.
A program may use at most 320 MiB of HBM per device.

v0:
```python
import math

import jax
import jax.numpy as jnp
from jax import lax
from jax.sharding import PartitionSpec as P

NLON = 3200
LEV = 64


precise = lax.Precision.HIGHEST
damping_rate = 4.0


def zonal_table(wave_ids, lon_ids):
    phase_index = wave_ids[:, None] * lon_ids[None, :] % NLON
    phase_angle = phase_index.astype(jnp.float32) * (2.0 * math.pi / NLON)
    return jnp.stack([jnp.cos(phase_angle), -jnp.sin(phase_angle)], axis=1).astype(jnp.bfloat16)


def on_device(fourier_rows, legendre, wavenumber, lower_diag, main_diag, upper_diag):
    lat_count = lax.axis_size("lat")
    wave_count = lax.axis_size("wave")
    lat_pos = lax.axis_index("lat")
    wave_pos = lax.axis_index("wave")
    group_slots, row_count, row_width = fourier_rows.shape
    slot_share = group_slots // lat_count
    pair_count = legendre.shape[2]
    lat_rows = 2 * pair_count
    half_width = row_width // 2
    arrived = lax.all_to_all(fourier_rows, "lat", split_axis=0, concat_axis=1, tiled=True).astype(
        jnp.float32
    )
    upper_half = arrived[:, :pair_count]
    lower_half = arrived[:, pair_count:]
    parity_parts = jnp.stack([upper_half + lower_half, upper_half - lower_half], axis=1)
    table_rows = lax.all_to_all(legendre, "lat", split_axis=0, concat_axis=1, tiled=True)
    table_parts = table_rows.reshape(slot_share, 2, pair_count, pair_count)
    spectral = jnp.einsum(
        "spcq,spqk->spck",
        table_parts,
        parity_parts,
        precision=precise,
        preferred_element_type=jnp.float32,
    )
    slot_first = wave_pos * group_slots + lat_pos * slot_share
    wave_ids = lax.dynamic_slice_in_dim(wavenumber, slot_first, slot_share)
    column_ids = jnp.arange(pair_count, dtype=jnp.int32)
    parity_ids = jnp.arange(2, dtype=jnp.int32)
    degree_int = wave_ids[:, None, None] + 2 * column_ids[None, None, :] + parity_ids[None, :, None]
    inside_mask = degree_int < lat_rows
    inside = inside_mask.astype(jnp.float32)
    degree = degree_int.astype(jnp.float32)
    degree_ratio = degree * (degree + 1.0) / (lat_rows * (lat_rows - 1.0))
    damping = 1.0 / (1.0 + damping_rate * degree_ratio * degree_ratio)
    spectral = spectral * inside[..., None]
    fields = spectral.reshape(slot_share, 2, pair_count, 2, 3, LEV)
    vorticity = fields[:, :, :, :, 0:1, :]
    div_temp = fields[:, :, :, :, 1:, :].reshape(slot_share, 2, pair_count, 4 * LEV)
    local_first = lat_pos * slot_share
    lower_band = lax.dynamic_slice_in_dim(lower_diag, local_first, slot_share, 0).reshape(
        slot_share, 2, pair_count
    )
    main_band = lax.dynamic_slice_in_dim(main_diag, local_first, slot_share, 0).reshape(
        slot_share, 2, pair_count
    )
    upper_band = lax.dynamic_slice_in_dim(upper_diag, local_first, slot_share, 0).reshape(
        slot_share, 2, pair_count
    )
    not_first = (column_ids > 0).astype(jnp.float32)
    not_last = (column_ids < pair_count - 1).astype(jnp.float32)
    sub_band = lower_band * inside * not_first
    super_band = upper_band * inside * not_last
    center = jnp.where(inside_mask, main_band, 1.0)
    solved = lax.linalg.tridiagonal_solve(sub_band, center, super_band, div_temp)
    merged = jnp.concatenate(
        [vorticity, solved.reshape(slot_share, 2, pair_count, 2, 2, LEV)], axis=4
    )
    merged = merged.reshape(slot_share, 2, pair_count, row_width) * damping[..., None]
    grid_parts = jnp.einsum(
        "spcq,spck->spqk",
        table_parts,
        merged,
        precision=precise,
        preferred_element_type=jnp.float32,
    )
    north_rows = grid_parts[:, 0] + grid_parts[:, 1]
    south_rows = grid_parts[:, 0] - grid_parts[:, 1]
    home_rows = jnp.concatenate([north_rows, south_rows], axis=1).astype(jnp.bfloat16)
    fourier_new = lax.all_to_all(home_rows, "lat", split_axis=1, concat_axis=0, tiled=True)
    lon_dev = NLON // wave_count
    lon_ids = wave_pos * lon_dev + jnp.arange(lon_dev, dtype=jnp.int32)
    piece_rows = lax.all_gather(fourier_new, "wave", axis=0, tiled=True)
    piece_count = piece_rows.shape[0]
    zonal_trig = zonal_table(wavenumber, lon_ids)
    spread = piece_rows.reshape(piece_count, row_count, 2, half_width)
    grid_sums = jnp.einsum("mcl,mrcj->lrj", zonal_trig, spread, preferred_element_type=jnp.float32)
    return grid_sums.astype(jnp.bfloat16).reshape(lon_dev, row_count * half_width)


def solution(mesh):
    placed = (
        P("wave", "lat", None),
        P("wave", "lat", None),
        P(),
        P("wave", None),
        P("wave", None),
        P("wave", None),
    )
    return jax.shard_map(
        on_device, mesh=mesh, in_specs=placed, out_specs=P("wave", "lat"), check_vma=False
    )
```

profile of v0, /device:TPU:0, one launch (start us, length us, event | category | flops | bytes accessed | tf_op | source)
XLA Modules:
  0.0 1986.4 jit_solution(9911280084395872405)
XLA Ops:
  6.5 62.2 %all_to_all.42 = bf16[32,200,384]{2,1,0:T(8,128)(2,1)} all-to-all(bf16[32,200,384]{2,1,0:T(8,128)(2,1)} %param.10), channel_id=1, replica_groups=mesh['lat'=8,'wave'=4] {'lat'}, dimensions={0} | all-to-all | bytes 9830400 | tf_op jit(solution)/shard_map/all_to_all | solution.py:32
  68.7 6.3 all-to-all-start.1
  147.4 4.5 copy.11580
  151.9 8.2 add_bitcast_fusion
  160.1 165.0 %all-to-all-done.1 = f32[32,200,800]{2,1,0:T(8,128)} async-done(((f32[32,200,800]{2,1,0:T(8,128)}), f32[32,200,800]{2,1,0:T(8,128)}, u32[]{:S(2)}, u32[]{:S(2)}) %all-to-all-start.1) | async-done | bytes 20480032 | tf_op jit(solution)/shard_map/all_to_all | solution.py:38
  325.1 8.4 copy.11582
  333.5 8.2 copy-done.2
  341.7 42.8 %multiply_bitcast_fusion = f32[4,2,800,384]{3,2,1,0:T(8,128)} fusion(f32[4,2,800]{2,1,0:T(2,128)S(1)} %get-tuple-element.1012, f32[4,2,800,800]{3,2,1,0:T(8,128)S(1)} %bitcast.2209, f32[4,1,800,384]{3,2,1,0:T(8,128)} %get-tuple-element.869, f32[4,1,800,384]{3,2,1,0:T(8,128)} %get-tuple-element.868), kind=kOutput, calls=%fused_computation.652 | convolution fusion | flops 23597875200 | bytes 40166400 | tf_op jit(solution)/shard_map/spcq,spqk->spck/dot_general | solution.py:40
  384.5 11.0 copy.11583
  395.5 4.2 slice.2164
  399.7 3.9 slice.2167
  406.0 6.7 slice_reduce_fusion.19
  412.7 11.1 slice_reduce_fusion
  427.0 6.5 copy.11587
  434.0 349.4 %while.32 = (s32[]{:T(128)}, f32[4,2]{0,1:T(2,128)S(1)}, f32[4,2,256]{2,1,0:T(2,128)S(1)}, f32[24,32,4,2]{2,3,1,0:T(2,128)}, f32[24,32,4,2,256]{4,3,2,1,0:T(2,12...) while((s32[]{:T(128)}, f32[4,2]{0,1:T(2,128)S(1)}, ...), condition=%wide.region_1.2_spmd, body=%wide.region_0.1_spmd.sunk | while | flops 295713 | bytes 2588137 | solution.py:76
  798.5 7.5 constant_dynamic-update-slice_fusion.128
  827.1 7.7 slice.2364
  834.9 3.4 broadcast.256.clone
  838.2 406.3 %while.33 = (s32[]{:T(128)}, f32[4,2,256]{2,1,0:T(2,128)S(1)}, f32[24,32,4,2,256]{4,1,0,3,2:T(8,128)}, f32[24,32,4,2,256]{4,3,2,1,0:T(2,128)}, f32[24,32,4,2]{2,...) while((s32[]{:T(128)}, f32[4,2,256]{2,1,0:T(2,128)S(1)}, ...), condition=%wide.region_3.4_spmd, body=%wide.region_2.3_spmd.sunk | while | flops 192545 | bytes 1632365 | solution.py:76
  1248.9 22.0 %concatenate.42 = f32[799,4,2,256]{3,0,2,1:T(8,128)} concatenate(f32[1,4,2,256]{3,0,2,1:T(1,128)S(1)} %copy.11811, f32[1,4,2,256]{3,0,2,1:T(1,128)S(1)} %copy.11812, f32[1,4,2,256]{3,0,2,1:T(1,128)S(1)} %copy.11813, f32[1,4,2,256]{3,0,2,1:T(1,128)S(1)} %copy.11814, f32[1,4,2,256]{3,0,2,1:T(1,128)S(1)} %copy.11815, f32[1,4,2,256]{3,0,2,1:T(1,128)S(1)} %copy.11816, ...), dimensions={0} | concatenate | bytes 13090816 | tf_op jit(solution)/shard_map/vmap(vmap())/concatenate | solution.py:76
  1270.9 7.5 copy.11841
  1279.3 10.5 maximum_maximum_fusion
  1289.8 5.0 bitcast_multiply_fusion
  1294.8 45.7 %convolution_bitcast_fusion = f32[4,2,800,384]{3,2,1,0:T(8,128)} fusion(f32[4,2,800,384]{2,3,1,0:T(8,128)S(1)} %bitcast_multiply_fusion, f32[4,2,800,800]{3,2,1,0:T(8,128)} %bitcast.2210), kind=kOutput, calls=%fused_computation.659 | convolution fusion | flops 23592960000 | bytes 40140800 | tf_op jit(solution)/shard_map/spcq,spck->spqk/dot_general | solution.py:81
  1340.4 4.8 fusion.327
  1345.8 25.3 %copy.11845 = bf16[4,1600,384]{2,0,1:T(4,128)(2,1)S(1)} copy(bf16[4,1600,384]{2,1,0:T(8,128)(2,1)S(1)} %pad_maximum_fusion) | data formatting | bytes 9830400 | tf_op jit(solution)/shard_map/concatenate | solution.py:90
  1371.1 59.5 %all_to_all.43 = bf16[4,1600,384]{2,0,1:T(4,128)(2,1)S(1)} all-to-all(bf16[4,1600,384]{2,0,1:T(4,128)(2,1)S(1)} %copy.11845), channel_id=1, replica_groups=mesh['lat'=8,'wave'=4] {'lat'}, dimensions={1} | all-to-all | bytes 9830400 | tf_op jit(solution)/shard_map/all_to_all | solution.py:91
  1436.2 333.5 %all-gather.2.cloned.1.call-done = bf16[128,200,384]{2,1,0:T(8,128)(2,1)} async-done(((bf16[32,200,384]{2,1,0:T(8,128)(2,1)}), bf16[128,200,384]{2,1,0:T(8,128)(2,1)}) %all-gather.2.cloned.1.call-update) | async-done | bytes 19660816 | tf_op jit(solution)/shard_map/all_gather | solution.py:94
  1769.7 27.4 %copy.11848 = bf16[128,200,384]{0,2,1:T(8,128)(2,1)} copy(bf16[128,200,384]{2,1,0:T(8,128)(2,1)} %all-gather.2.cloned.1.call-done) | data formatting | bytes 39321600 | tf_op jit(solution)/shard_map/all_gather | solution.py:94
  1797.0 45.9 %bitcast_convert_fusion = bf16[800,200,192]{0,1,2:T(8,128)(2,1)} fusion(bf16[128,200,2,192]{0,3,2,1:T(8,128)(2,1)} %bitcast.2211, bf16[128,1,800]{0,2,1:T(8,128)(2,1)S(1)} %get-tuple-element.1014, bf16[128,1,800]{0,2,1:T(8,128)(2,1)S(1)} %get-tuple-element.1013), kind=kOutput, calls=%fused_computation.643 | convolution fusion | flops 15760179200 | bytes 81510400 | tf_op jit(solution)/shard_map/mcl,mrcj->lrj/dot_general | solution.py:98
  1842.9 56.1 %copy.11850 = bf16[800,200,192]{0,2,1:T(8,128)(2,1)} copy(bf16[800,200,192]{0,1,2:T(8,128)(2,1)} %bitcast_convert_fusion) | data formatting | bytes 122880000 | tf_op jit(solution)/shard_map/convert_element_type | solution.py:99
  1899.0 80.3 %copy.11851 = bf16[800,38400]{1,0:T(8,128)(2,1)} copy(bf16[800,38400]{0,1:T(8,128)(2,1)} %bitcast.577) | data formatting | bytes 122880000 | tf_op jit(solution)/shard_map/reshape | solution.py:99
  (5432 shorter events, 872.1 us)
Async XLA Ops:
  68.7 256.3 %all-to-all-start.1 = ((f32[32,200,800]{2,1,0:T(8,128)}), f32[32,200,800]{2,1,0:T(8,128)}, u32[]{:S(2)}, u32[]{:S(2)}) async-start(f32[32,200,800]{2,1,0:T(8,128)} %param.11), calls=%async_computation.1 | async-start | bytes 45875200 | tf_op jit(solution)/shard_map/all_to_all | solution.py:38
  75.1 1694.6 %all-gather.2.cloned.1.call-start = ((), (), s32[]{:S(2)}) async-start(), calls=%async_computation.3 | async-start | bytes 24576000 | tf_op jit(solution)/shard_map/all_gather | solution.py:94
  433.6 352.6 %copy-start.22 = (f32[1,4,2]{1,2,0:T(2,128)S(1)}, f32[1,4,2]{1,2,0:T(2,128)}, u32[]{:S(2)}) copy-start(f32[1,4,2]{1,2,0:T(2,128)} %copy-done.21) | copy-start | bytes 100
  433.6 352.6 %copy-start.26 = (f32[1,4,2]{1,2,0:T(2,128)S(1)}, f32[1,4,2]{1,2,0:T(2,128)}, u32[]{:S(2)}) copy-start(f32[1,4,2]{1,2,0:T(2,128)} %copy-done.25) | copy-start | bytes 100
  433.6 352.6 %copy-start.28 = (f32[1,4,2]{1,2,0:T(2,128)S(1)}, f32[1,4,2]{1,2,0:T(2,128)}, u32[]{:S(2)}) copy-start(f32[1,4,2]{1,2,0:T(2,128)} %copy-done.27) | copy-start | bytes 100
  433.6 352.6 %copy-start.30 = (f32[1,4,2]{1,2,0:T(2,128)S(1)}, f32[1,4,2]{1,2,0:T(2,128)}, u32[]{:S(2)}) copy-start(f32[1,4,2]{1,2,0:T(2,128)} %copy-done.29) | copy-start | bytes 100
  433.6 352.6 %copy-start.32 = (f32[1,4,2]{1,2,0:T(2,128)S(1)}, f32[1,4,2]{1,2,0:T(2,128)}, u32[]{:S(2)}) copy-start(f32[1,4,2]{1,2,0:T(2,128)} %copy-done.31) | copy-start | bytes 100
  433.6 352.6 %copy-start.34 = (f32[1,4,2]{1,2,0:T(2,128)S(1)}, f32[1,4,2]{1,2,0:T(2,128)}, u32[]{:S(2)}) copy-start(f32[1,4,2]{1,2,0:T(2,128)} %copy-done.33) | copy-start | bytes 100
  433.6 352.6 %copy-start.36 = (f32[1,4,2]{1,2,0:T(2,128)S(1)}, f32[1,4,2]{1,2,0:T(2,128)}, u32[]{:S(2)}) copy-start(f32[1,4,2]{1,2,0:T(2,128)} %copy-done.35) | copy-start | bytes 100
  433.7 352.6 %copy-start.38 = (f32[1,4,2]{1,2,0:T(2,128)S(1)}, f32[1,4,2]{1,2,0:T(2,128)}, u32[]{:S(2)}) copy-start(f32[1,4,2]{1,2,0:T(2,128)} %copy-done.37) | copy-start | bytes 100
  433.7 352.6 %copy-start.40 = (f32[1,4,2]{1,2,0:T(2,128)S(1)}, f32[1,4,2]{1,2,0:T(2,128)}, u32[]{:S(2)}) copy-start(f32[1,4,2]{1,2,0:T(2,128)} %copy-done.39) | copy-start | bytes 100
  433.7 352.6 %copy-start.42 = (f32[1,4,2]{1,2,0:T(2,128)S(1)}, f32[1,4,2]{1,2,0:T(2,128)}, u32[]{:S(2)}) copy-start(f32[1,4,2]{1,2,0:T(2,128)} %copy-done.41) | copy-start | bytes 100
  433.7 352.6 %copy-start.44 = (f32[1,4,2]{1,2,0:T(2,128)S(1)}, f32[1,4,2]{1,2,0:T(2,128)}, u32[]{:S(2)}) copy-start(f32[1,4,2]{1,2,0:T(2,128)} %copy-done.43) | copy-start | bytes 100
  433.7 352.6 %copy-start.46 = (f32[1,4,2]{1,2,0:T(2,128)S(1)}, f32[1,4,2]{1,2,0:T(2,128)}, u32[]{:S(2)}) copy-start(f32[1,4,2]{1,2,0:T(2,128)} %copy-done.45) | copy-start | bytes 100
  433.7 352.6 %copy-start.48 = (f32[1,4,2]{1,2,0:T(2,128)S(1)}, f32[1,4,2]{1,2,0:T(2,128)}, u32[]{:S(2)}) copy-start(f32[1,4,2]{1,2,0:T(2,128)} %copy-done.47) | copy-start | bytes 100
  433.7 352.6 %copy-start.50 = (f32[1,4,2]{1,2,0:T(2,128)S(1)}, f32[1,4,2]{1,2,0:T(2,128)}, u32[]{:S(2)}) copy-start(f32[1,4,2]{1,2,0:T(2,128)} %copy-done.49) | copy-start | bytes 100
  433.7 352.6 %copy-start.52 = (f32[1,4,2]{1,2,0:T(2,128)S(1)}, f32[1,4,2]{1,2,0:T(2,128)}, u32[]{:S(2)}) copy-start(f32[1,4,2]{1,2,0:T(2,128)} %copy-done.51) | copy-start | bytes 100
  433.7 352.6 %copy-start.54 = (f32[1,4,2]{1,2,0:T(2,128)S(1)}, f32[1,4,2]{1,2,0:T(2,128)}, u32[]{:S(2)}) copy-start(f32[1,4,2]{1,2,0:T(2,128)} %copy-done.53) | copy-start | bytes 100
  433.7 352.6 %copy-start.56 = (f32[1,4,2]{1,2,0:T(2,128)S(1)}, f32[1,4,2]{1,2,0:T(2,128)}, u32[]{:S(2)}) copy-start(f32[1,4,2]{1,2,0:T(2,128)} %copy-done.55) | copy-start | bytes 100
  433.8 352.6 %copy-start.58 = (f32[1,4,2]{1,2,0:T(2,128)S(1)}, f32[1,4,2]{1,2,0:T(2,128)}, u32[]{:S(2)}) copy-start(f32[1,4,2]{1,2,0:T(2,128)} %copy-done.57) | copy-start | bytes 100
  433.8 352.6 %copy-start.60 = (f32[1,4,2]{1,2,0:T(2,128)S(1)}, f32[1,4,2]{1,2,0:T(2,128)}, u32[]{:S(2)}) copy-start(f32[1,4,2]{1,2,0:T(2,128)} %copy-done.59) | copy-start | bytes 100
  433.8 352.6 %copy-start.62 = (f32[1,4,2]{1,2,0:T(2,128)S(1)}, f32[1,4,2]{1,2,0:T(2,128)}, u32[]{:S(2)}) copy-start(f32[1,4,2]{1,2,0:T(2,128)} %copy-done.61) | copy-start | bytes 100
  433.8 352.6 %copy-start.64 = (f32[1,4,2]{1,2,0:T(2,128)S(1)}, f32[1,4,2]{1,2,0:T(2,128)}, u32[]{:S(2)}) copy-start(f32[1,4,2]{1,2,0:T(2,128)} %copy-done.63) | copy-start | bytes 100
  433.8 352.6 %copy-start.66 = (f32[1,4,2]{1,2,0:T(2,128)S(1)}, f32[1,4,2]{1,2,0:T(2,128)}, u32[]{:S(2)}) copy-start(f32[1,4,2]{1,2,0:T(2,128)} %copy-done.65) | copy-start | bytes 100
  433.8 352.6 %copy-start.68 = (f32[1,4,2]{1,2,0:T(2,128)S(1)}, f32[1,4,2]{1,2,0:T(2,128)}, u32[]{:S(2)}) copy-start(f32[1,4,2]{1,2,0:T(2,128)} %copy-done.67) | copy-start | bytes 100
  433.8 352.6 %copy-start.70 = (f32[1,4,2]{1,2,0:T(2,128)S(1)}, f32[1,4,2]{1,2,0:T(2,128)}, u32[]{:S(2)}) copy-start(f32[1,4,2]{1,2,0:T(2,128)} %copy-done.69) | copy-start | bytes 100
  433.8 352.6 %copy-start.72 = (f32[1,4,2]{1,2,0:T(2,128)S(1)}, f32[1,4,2]{1,2,0:T(2,128)}, u32[]{:S(2)}) copy-start(f32[1,4,2]{1,2,0:T(2,128)} %copy-done.71) | copy-start | bytes 100
  433.8 352.6 %copy-start.74 = (f32[1,4,2]{1,2,0:T(2,128)S(1)}, f32[1,4,2]{1,2,0:T(2,128)}, u32[]{:S(2)}) copy-start(f32[1,4,2]{1,2,0:T(2,128)} %copy-done.73) | copy-start | bytes 100
  433.8 352.6 %copy-start.76 = (f32[1,4,2]{1,2,0:T(2,128)S(1)}, f32[1,4,2]{1,2,0:T(2,128)}, u32[]{:S(2)}) copy-start(f32[1,4,2]{1,2,0:T(2,128)} %copy-done.75) | copy-start | bytes 100
  433.9 352.6 %copy-start.78 = (f32[1,4,2]{1,2,0:T(2,128)S(1)}, f32[1,4,2]{1,2,0:T(2,128)}, u32[]{:S(2)}) copy-start(f32[1,4,2]{1,2,0:T(2,128)} %copy-done.77) | copy-start | bytes 100
  433.9 352.6 %copy-start.80 = (f32[1,4,2]{1,2,0:T(2,128)S(1)}, f32[1,4,2]{1,2,0:T(2,128)}, u32[]{:S(2)}) copy-start(f32[1,4,2]{1,2,0:T(2,128)} %copy-done.79) | copy-start | bytes 100
  433.9 352.6 %copy-start.82 = (f32[1,4,2]{1,2,0:T(2,128)S(1)}, f32[1,4,2]{1,2,0:T(2,128)}, u32[]{:S(2)}) copy-start(f32[1,4,2]{1,2,0:T(2,128)} %copy-done.81) | copy-start | bytes 100
  (81 other events, 4665.4 us)
Sparse Core Ops, SparseCore 0:
  1434.1 335.4 all-gather.1
where the time goes:
time: 2020 us; the launch traced here: 1990 us
  local copies, waits for them, and re-layouts  752 us (37%)
  waiting for transfers between devices  499 us (25%)
  other arithmetic  450 us (22%)
  matrix products  134 us (7%)
  blocking collectives  122 us (6%)
    while x1800, other arithmetic  366 us
    all_gather x1, waiting for transfers between devices, on_device(): piece_rows = lax.all_gather(fourier_new, 'wave', axis=0, tiled=True)  333 us
    slice x162, local copies, waits for them, and re-layouts, on_device(): lax.linalg.tridiagonal_solve(sub_band, center, super_band, div_temp)  170 us
    all_to_all x1, waiting for transfers between devices, on_device(): lax.all_to_all(legendre, 'lat', split_axis=0, concat_axis=1, tiled=True)  165 us
    mul x880, local copies, waits for them, and re-layouts, on_device(): lax.linalg.tridiagonal_solve(sub_band, center, super_band, div_temp)  96.4 us
    reshape x1, local copies, waits for them, and re-layouts, on_device(): grid_sums.astype(jnp.bfloat16).reshape(lon_dev, row_count * half_width)  80.3 us
    sub x799, local copies, waits for them, and re-layouts, on_device(): lax.linalg.tridiagonal_solve(sub_band, center, super_band, div_temp)  74.8 us
    squeeze x769, local copies, waits for them, and re-layouts, on_device(): lax.linalg.tridiagonal_solve(sub_band, center, super_band, div_temp)  71.4 us

commit v1 on v0

v1 whole, which is shorter than its diff:
```python
import functools
import math

import jax
import jax.numpy as jnp
from jax import lax
from jax.experimental import pallas as pl
from jax.experimental.pallas import tpu as pltpu
from jax.sharding import PartitionSpec as P

NLON = 3200
LEV = 64
damping_rate = 4.0
BLOCKS = 8
VMEM_LIMIT = 56 * 2**20
f32 = jnp.float32
bf16 = jnp.bfloat16


def zonal_matrix(wave_ids, lon_ids):
    phase_index = lon_ids[:, None, None] * wave_ids[None] % NLON
    phase_angle = phase_index.astype(f32) * (2.0 * math.pi / NLON)
    table = jnp.stack([jnp.cos(phase_angle), -jnp.sin(phase_angle)], axis=2).astype(bf16)
    return table.reshape(lon_ids.shape[0], 2 * wave_ids.size)


def factor_kernel(bands_ref, factors_ref, links_ref):
    systems, _, _, steps = bands_ref.shape
    sub, center, sup, inside, damping = (bands_ref[:, n] for n in range(5))
    lanes = lax.broadcasted_iota(jnp.int32, (systems, BLOCKS, steps), 2)

    def column(values, i):
        return values[:, :, i : i + 1]

    def place(values, i, new):
        return jnp.where(lanes == i, new, values)

    zero = jnp.zeros((systems, BLOCKS, steps), f32)
    inv, scaled_sub, scaled_sup, left, right = zero, zero, zero, zero, zero
    for i in range(steps):
        pivot = column(center, i)
        if i:
            pivot = pivot - column(sub, i) * sup_part
        inv_part = 1.0 / pivot
        sub_part = column(sub, i) * inv_part
        sup_part = column(sup, i) * inv_part
        left_part = -sub_part * left_part if i else sub_part
        inv = place(inv, i, inv_part)
        scaled_sub = place(scaled_sub, i, sub_part)
        scaled_sup = place(scaled_sup, i, sup_part)
        left = place(left, i, left_part)
    solved_left = zero
    for i in reversed(range(steps)):
        if i == steps - 1:
            right_part = column(scaled_sup, i)
            left_part = column(left, i)
        else:
            right_part = -column(scaled_sup, i) * right_part
            left_part = column(left, i) - column(scaled_sup, i) * left_part
        right = place(right, i, right_part)
        solved_left = place(solved_left, i, left_part)
    for n, values in enumerate((inv * inside, scaled_sub, scaled_sup, right, solved_left, damping * inside)):
        factors_ref[:, n] = values
    right_first, right_last = column(right, 0), column(right, steps - 1)
    left_first, left_last = column(solved_left, 0), column(solved_left, steps - 1)
    beta = jnp.zeros((systems, 1, 1), f32)
    width = links_ref.shape[-1]
    for b in range(BLOCKS):
        row = slice(b, b + 1)
        scale = 1.0 / (1.0 - left_first[:, row] * beta)
        step = right_first[:, row] * scale
        across = left_last[:, row] * beta
        beta = right_last[:, row] + across * step
        for n, value in enumerate((scale, left_first[:, row] * scale, step, left_last[:, row], across, beta)):
            links_ref[:, n, b : b + 1, :] = jnp.broadcast_to(value, (systems, 1, width))


def wave_kernel(arrived_ref, factors_ref, links_ref, home_ref, spec, part):
    _, pair_count, width = home_ref.shape
    steps = pair_count // BLOCKS
    tiles = width // 128
    north = arrived_ref[0, :, :width].astype(f32)
    south = arrived_ref[1, :, :width].astype(f32)
    for p in range(2):
        folded = (north + south if p == 0 else north - south).astype(bf16)
        spectral = jnp.dot(arrived_ref[p, :, width:], folded, preferred_element_type=f32)
        for t in range(tiles):
            spec[p, t] = spectral[:, 128 * t : 128 * t + 128]

    def spec_rows(p, i):
        return jnp.concatenate([spec[p, t, pl.ds(i, BLOCKS, stride=steps), :] for t in range(tiles)], axis=1)

    def factor(p, n, i):
        return factors_ref[p, n, :, i : i + 1]

    running = [None, None]
    for i in range(steps):
        for p in range(2):
            value = spec_rows(p, i) * factor(p, 0, i)
            if i:
                value = value - factor(p, 1, i) * running[p]
            part[p, i] = value
            running[p] = value
    last = list(running)
    for i in reversed(range(steps - 1)):
        for p in range(2):
            value = part[p, i] - factor(p, 2, i) * running[p]
            part[p, i] = value
            running[p] = value
    first = running
    after, before = [], []
    for p in range(2):
        def link(n, b):
            return jnp.concatenate([links_ref[p, n, b : b + 1, :]] * tiles, axis=1)

        alpha = jnp.zeros((1, width), f32)
        heads, tails = [], []
        for b in range(BLOCKS):
            row = slice(b, b + 1)
            head = first[p][row] * link(0, b) - link(1, b) * alpha
            alpha = last[p][row] - link(3, b) * alpha + link(4, b) * head
            heads.append(head)
            tails.append(alpha)
        ahead = jnp.zeros((1, width), f32)
        next_heads, prev_tails = [None] * BLOCKS, [jnp.zeros((1, width), f32)] * BLOCKS
        for b in reversed(range(BLOCKS)):
            next_heads[b] = ahead
            if b + 1 < BLOCKS:
                prev_tails[b + 1] = tails[b] - link(5, b) * ahead
            ahead = heads[b] - link(2, b) * ahead
        after.append(jnp.concatenate(next_heads, axis=0))
        before.append(jnp.concatenate(prev_tails, axis=0))
    half = lax.broadcasted_iota(jnp.int32, (BLOCKS, width), 1) % (width // 2)
    untouched = half < LEV
    for i in range(steps):
        for p in range(2):
            solved = part[p, i] - factor(p, 3, i) * after[p] - factor(p, 4, i) * before[p]
            damped = jnp.where(untouched, spec_rows(p, i), solved) * factor(p, 5, i)
            for t in range(tiles):
                spec[p, t, pl.ds(i, BLOCKS, stride=steps), :] = damped[:, 128 * t : 128 * t + 128]
    parts = []
    for p in range(2):
        damped = jnp.concatenate([spec[p, t].astype(bf16) for t in range(tiles)], axis=1)
        parts.append(
            lax.dot_general(
                arrived_ref[p, :, width:], damped, (((0,), (0,)), ((), ())), preferred_element_type=f32
            )
        )
    home_ref[0] = (parts[0] + parts[1]).astype(bf16)
    home_ref[1] = (parts[0] - parts[1]).astype(bf16)


def pair_kernel(rows_ref, pairs_ref):
    slots, groups, rows, width = rows_ref.shape
    order = slots * rows
    out_row = lax.broadcasted_iota(jnp.int32, (order, order), 0)
    in_row = lax.broadcasted_iota(jnp.int32, (order, order), 1)
    odd, rest = out_row // (order // 2), out_row % (order // 2)
    source = (rest % slots) * rows + 2 * (rest // slots) + odd
    shuffle = (in_row == source).astype(bf16)
    first_half = lax.broadcasted_iota(jnp.int32, (order // 2, width), 1) < width // 2

    def swap(values):
        return jnp.concatenate([values[:, width // 2 :], values[:, : width // 2]], axis=1)

    def one(g, _):
        block = rows_ref[:, g].astype(f32).reshape(order, width).astype(bf16)
        moved = jnp.dot(shuffle, block, preferred_element_type=f32)
        even_rows, odd_rows = moved[: order // 2], moved[order // 2 :]
        real = jnp.where(first_half, even_rows, swap(odd_rows)).reshape(rows // 2, slots, width)
        imag = jnp.where(first_half, swap(even_rows), odd_rows).reshape(rows // 2, slots, width)
        pairs_ref[pl.ds(g * (rows // 2), rows // 2)] = jnp.concatenate([real, imag], axis=1).astype(bf16)
        return 0

    lax.fori_loop(0, groups, one, 0)


def zonal_kernel(chunks, trig_ref, *refs):
    grid_ref = refs[-1]
    waves, pairs, depth, width = refs[0].shape
    for r in range(0, pairs, 2):
        rhs = jnp.concatenate(
            [
                jnp.concatenate([refs[j][z, r + n] for j in range(chunks) for z in range(waves)], axis=0)
                for n in range(2)
            ],
            axis=1,
        )
        sums = jnp.dot(trig_ref[...], rhs, preferred_element_type=f32)
        grid_ref[:, r * width : (r + 2) * width] = sums.astype(bf16)


def params():
    return pltpu.CompilerParams(vmem_limit_bytes=VMEM_LIMIT)


def whole_vmem(count):
    return [pl.BlockSpec(memory_space=pltpu.VMEM)] * count


def make_factors(bands):
    systems, _, _, steps = bands.shape
    return pl.pallas_call(
        factor_kernel,
        out_shape=(
            jax.ShapeDtypeStruct((systems, 6, BLOCKS, steps), f32),
            jax.ShapeDtypeStruct((systems, 6, BLOCKS, 128), f32),
        ),
        in_specs=whole_vmem(1),
        out_specs=tuple(whole_vmem(2)),
        compiler_params=params(),
        cost_estimate=pl.CostEstimate(flops=2_000_000_000, bytes_accessed=2_000_000, transcendentals=0),
        name="factor",
    )(bands)


def wave_step(arrived, factors, links, width):
    _, pair_count, _ = arrived.shape
    return pl.pallas_call(
        wave_kernel,
        out_shape=jax.ShapeDtypeStruct((2, pair_count, width), bf16),
        in_specs=whole_vmem(3),
        out_specs=whole_vmem(1)[0],
        scratch_shapes=[
            pltpu.VMEM((2, width // 128, pair_count, 128), f32),
            pltpu.VMEM((2, pair_count // BLOCKS, BLOCKS, width), f32),
        ],
        compiler_params=params(),
        cost_estimate=pl.CostEstimate(flops=8_000_000_000, bytes_accessed=6_000_000, transcendentals=0),
        name="wave",
    )(arrived, factors, links)


def pair_rows(rows):
    slots, count, width = rows.shape
    if count % 8 or slots % 8:
        split = rows.reshape(slots, count // 2, 2, 2, width // 2)
        return split.transpose(1, 3, 0, 2, 4).reshape(count // 2, 2 * slots, width)
    return pl.pallas_call(
        pair_kernel,
        out_shape=jax.ShapeDtypeStruct((count // 2, 2 * slots, width), bf16),
        in_specs=whole_vmem(1),
        out_specs=whole_vmem(1)[0],
        compiler_params=params(),
        cost_estimate=pl.CostEstimate(flops=2_000_000_000, bytes_accessed=2_400_000, transcendentals=0),
        name="pair",
    )(rows.reshape(slots, count // 8, 8, width))


def synthesize(trig, gathered):
    lons, depth = trig.shape
    waves, pairs, rows, width = gathered[0].shape
    step = next(n for n in (4, 2, 1) if pairs % n == 0)
    assert step > 1
    spec = pl.BlockSpec((waves, step, rows, width), lambda i: (0, i, 0, 0))
    return pl.pallas_call(
        functools.partial(zonal_kernel, len(gathered)),
        out_shape=jax.ShapeDtypeStruct((lons, pairs * width), bf16),
        grid=(pairs // step,),
        in_specs=[pl.BlockSpec((lons, depth), lambda i: (0, 0))] + [spec] * len(gathered),
        out_specs=pl.BlockSpec((lons, step * width), lambda i: (0, i)),
        compiler_params=params(),
        cost_estimate=pl.CostEstimate(
            flops=2 * lons * depth * pairs * width, bytes_accessed=2 * lons * pairs * width, transcendentals=0
        ),
        name="zonal",
    )(trig, *gathered)


def on_device(fourier_rows, legendre, wavenumber, lower_diag, main_diag, upper_diag):
    lat_count = lax.axis_size("lat")
    wave_count = lax.axis_size("wave")
    lat_pos = lax.axis_index("lat")
    wave_pos = lax.axis_index("wave")
    group_slots, row_count, row_width = fourier_rows.shape
    pair_count = legendre.shape[2]
    lat_rows = 2 * pair_count
    chunks = group_slots // lat_count
    steps = pair_count // BLOCKS

    slot_ids = wavenumber.reshape(wave_count, chunks, lat_count)
    own_group = lax.dynamic_index_in_dim(slot_ids, wave_pos, 0, keepdims=False)
    wave_ids = lax.dynamic_index_in_dim(own_group, lat_pos, 1, keepdims=False)

    def own(band):
        return lax.dynamic_index_in_dim(
            band.reshape(chunks, lat_count, 2, pair_count), lat_pos, 1, keepdims=False
        )

    column_ids = jnp.arange(pair_count, dtype=jnp.int32)
    parity_ids = jnp.arange(2, dtype=jnp.int32)
    degree_int = wave_ids[:, None, None] + 2 * column_ids[None, None, :] + parity_ids[None, :, None]
    inside_mask = degree_int < lat_rows
    inside = inside_mask.astype(f32)
    degree = degree_int.astype(f32)
    degree_ratio = degree * (degree + 1.0) / (lat_rows * (lat_rows - 1.0))
    damping = 1.0 / (1.0 + damping_rate * degree_ratio * degree_ratio)
    not_first = (column_ids > 0).astype(f32)
    not_last = (column_ids < pair_count - 1).astype(f32)
    sub_band = own(lower_diag) * inside * not_first
    super_band = own(upper_diag) * inside * not_last
    center = jnp.where(inside_mask, own(main_diag), 1.0)
    bands = jnp.stack([sub_band, center, super_band, inside, damping], axis=2)
    factors, links = make_factors(bands.reshape(2 * chunks, 5, BLOCKS, steps))
    factors = factors.reshape(chunks, 2, 6, BLOCKS, steps)
    links = links.reshape(chunks, 2, 6, BLOCKS, 128)

    gathered = []
    ready = None
    for j in range(chunks):
        pick = slice(j * lat_count, (j + 1) * lat_count)
        outgoing = jnp.concatenate([fourier_rows[pick], legendre[pick].astype(bf16)], axis=2)
        if ready is not None:
            outgoing, _ = lax.optimization_barrier((outgoing, ready))
        arrived = lax.all_to_all(outgoing, "lat", split_axis=0, concat_axis=0, tiled=True)
        arrived = arrived.reshape(2, pair_count, row_width + pair_count)
        home = wave_step(arrived, factors[j], links[j], row_width)
        home = home.reshape(lat_count, row_count, row_width)
        rows = lax.all_to_all(home, "lat", split_axis=0, concat_axis=0, tiled=True)
        ready = pair_rows(rows)
        gathered.append(lax.all_gather(ready, "wave", axis=0))

    lon_dev = NLON // wave_count
    lon_ids = wave_pos * lon_dev + jnp.arange(lon_dev, dtype=jnp.int32)
    trig = zonal_matrix(slot_ids.transpose(1, 0, 2).reshape(chunks * wave_count, lat_count), lon_ids)
    return synthesize(trig, gathered)


def solution(mesh):
    placed = (
        P("wave", "lat", None),
        P("wave", "lat", None),
        P(),
        P("wave", None),
        P("wave", None),
        P("wave", None),
    )
    return jax.shard_map(
        on_device, mesh=mesh, in_specs=placed, out_specs=P("wave", "lat"), check_vma=False
    )
```

time: 2020 us -> 530 us (0.26); the launches traced: 1990 us -> 529 us
  local copies, waits for them, and re-layouts: 752 us -> 16 us
  other arithmetic: 450 us -> 21.4 us
  waiting for transfers between devices: 499 us -> 113 us
  matrix products: 134 us -> 0 us
  Pallas kernels: 0 us -> 119 us
  blocking collectives: 122 us -> 240 us
    while x1800 -> x0, other arithmetic: 366 us -> none
    all_gather x1 -> x4, waiting for transfers between devices: 333 us -> 96.4 us  [on_device(): gathered.append(lax.all_gather(ready, 'wave', axis=0))]
    slice x164 -> x4, local copies, waits for them, and re-layouts: 178 us -> 10.5 us  [the longest x1 4.34 us: on_device(): fourier_rows[pick]]
    all_to_all x1, waiting for transfers between devices: 165 us -> 17 us  [on_device(): lax.all_to_all(outgoing, 'lat', split_axis=0, concat_axis=0, tiled=True)]
    dot_general x3 -> x0, matrix products: 134 us -> none  [the longest x1 45.9 us: on_device(): jnp.einsum('mcl,mrcj->lrj', zonal_trig, spread, preferred_element_type=jn...]
    pallas_call x0 -> x10, Pallas kernels: none -> 119 us  [the longest x1 36.3 us: synthesize(): pl.pallas_call(functools.partial(zonal_kernel, len(gathered)), out_shape=...]
    all_to_all x2 -> x7, blocking collectives: 122 us -> 240 us  [the longest x3 154 us: on_device(): lax.all_to_all(outgoing, 'lat', split_axis=0, concat_axis=0, tiled=True)]
    mul x881 -> x0, local copies, waits for them, and re-layouts: 107 us -> none  [the longest x880 96.4 us: on_device(): lax.linalg.tridiagonal_solve(sub_band, center, super_band, div_temp)]
where the time goes in v1:
time: 530 us; the launch traced here: 529 us
  blocking collectives  240 us (45%)
  Pallas kernels  119 us (22%)
  waiting for transfers between devices  113 us (21%)
  other arithmetic  21.4 us (4%)
  local copies, waits for them, and re-layouts  16 us (3%)
  between operations  13.3 us (3%)
  starting transfers between devices  5.46 us (1%)
    all_to_all x3, blocking collectives, on_device(): lax.all_to_all(outgoing, 'lat', split_axis=0, concat_axis=0, tiled=True)  154 us
    all_gather x4, waiting for transfers between devices, on_device(): gathered.append(lax.all_gather(ready, 'wave', axis=0))  96.4 us
    all_to_all x4, blocking collectives, on_device(): rows = lax.all_to_all(home, 'lat', split_axis=0, concat_axis=0, tiled=True)  86.2 us
    pallas_call x1, Pallas kernels, synthesize(): pl.pallas_call(functools.partial(zonal_kernel, len(gathered)), out_shape=...  36.3 us
    pallas_call x4, Pallas kernels, pair_rows(): pl.pallas_call(pair_kernel, out_shape=jax.ShapeDtypeStruct((count // 2, 2...  31.3 us
    pallas_call x4, Pallas kernels, wave_step(): pl.pallas_call(wave_kernel, out_shape=jax.ShapeDtypeStruct((2, pair_count...  29.7 us
    pallas_call x1, Pallas kernels, make_factors(): pl.pallas_call(factor_kernel, out_shape=(jax.ShapeDtypeStruct((systems, 6...  21.6 us
    all_to_all x1, waiting for transfers between devices, on_device(): lax.all_to_all(outgoing, 'lat', split_axis=0, concat_axis=0, tiled=True)  17 us
  transfers between devices with their start and end apart: 5, of which 3 were waited for; matrix products, arithmetic and copies ran while one was open for 3% of the time, Pallas kernels for 13%

profile of v1, /device:TPU:0, one launch (start us, length us, event | category | flops | bytes accessed | tf_op | source)
XLA Modules:
  0.0 528.6 jit_solution(133110126382424276)
XLA Ops:
  6.5 4.3 fusion.10
  10.9 8.3 %convert.14 = bf16[32,200,800]{2,1,0:T(8,128)(2,1)S(1)} convert(f32[32,200,800]{2,1,0:T(8,128)} %param.7) | non-fusion elementwise | flops 5120000 | bytes 30720000 | tf_op jit(solution)/shard_map/convert.3
  19.2 3.1 fusion.9
  22.2 2.4 pad_maximum_fusion
  24.6 5.3 %all-to-all-start = ((bf16[8,200,1184]{2,1,0:T(8,128)(2,1)}), bf16[8,200,1184]{2,1,0:T(8,128)(2,1)}, u32[]{:S(2)}, u32[]{:S(2)}) async-start(bf16[8,200,1184]{2,1,0:T(8,128)(2,1)} %pad_maximum_fusion), calls=%async_computation | async-start | bytes 8192000 | tf_op jit(solution)/shard_map/all_to_all | solution.py:315
  32.6 1.1 reshape.284
  36.3 21.6 %factor.1 = (f32[8,6,8,100]{3,2,1,0:T(8,128)}, f32[8,6,8,128]{3,2,1,0:T(8,128)}) custom-call(f32[8,5,8,100]{3,2,1,0:T(8,128)} %copy-done.4), custom_call_target="tpu_custom_call" | custom-call | flops 2000000000 | bytes 2000000 | tf_op jit(solution)/shard_map/factor/pallas_call | solution.py:203
  57.9 1.6 fusion.12
  59.5 1.6 fusion.11
  61.1 17.0 %all-to-all-done = bf16[8,200,1184]{2,1,0:T(8,128)(2,1)} async-done(((bf16[8,200,1184]{2,1,0:T(8,128)(2,1)}), bf16[8,200,1184]{2,1,0:T(8,128)(2,1)}, u32[]{:S(2)}, u32[]{:S(2)}) %all-to-all-start) | async-done | bytes 3788832 | tf_op jit(solution)/shard_map/all_to_all | solution.py:315
  78.1 7.5 %wave.4 = bf16[2,800,384]{2,1,0:T(8,128)(2,1)} custom-call(bf16[2,800,1184]{2,1,0:T(8,128)(2,1)} %bitcast.3.arrived_ref, f32[2,6,8,100]{3,2,1,0:T(8,128)} %get-tuple-element.32.factors_ref, f32[2,6,8,128]{3,2,1,0:T(8,128)} %get-tuple-element.28.links_ref), custom_call_target="tpu_custom_call" | custom-call | flops 8000000000 | bytes 6000000 | tf_op jit(solution)/shard_map/wave/pallas_call | solution.py:219
  85.6 21.5 %all_to_all.40 = bf16[8,200,384]{2,1,0:T(8,128)(2,1)} all-to-all(bf16[8,200,384]{2,1,0:T(8,128)(2,1)} %bitcast.39), channel_id=1, replica_groups=mesh['lat'=8,'wave'=4] {'lat'}, dimensions={0} | all-to-all | bytes 2457600 | tf_op jit(solution)/shard_map/all_to_all | solution.py:319
  107.1 7.8 %pair.4 = bf16[100,16,384]{2,1,0:T(8,128)(2,1)} custom-call(bf16[8,25,8,384]{3,2,1,0:T(8,128)(2,1)} %bitcast.43), custom_call_target="tpu_custom_call" | custom-call | flops 2000000000 | bytes 2400000 | tf_op jit(solution)/shard_map/pair/pallas_call | solution.py:239
  115.0 2.5 pad_maximum_fusion.1
  117.6 51.3 %all_to_all.41 = bf16[8,200,1184]{2,1,0:T(8,128)(2,1)} all-to-all(bf16[8,200,1184]{2,1,0:T(8,128)(2,1)S(1)} %pad_maximum_fusion.1), channel_id=1, replica_groups=mesh['lat'=8,'wave'=4] {'lat'}, dimensions={0} | all-to-all | bytes 7577600 | tf_op jit(solution)/shard_map/all_to_all | solution.py:315
  168.8 7.4 %wave.5 = bf16[2,800,384]{2,1,0:T(8,128)(2,1)} custom-call(bf16[2,800,1184]{2,1,0:T(8,128)(2,1)} %bitcast.36, f32[2,6,8,100]{3,2,1,0:T(8,128)} %get-tuple-element.31.factors_ref, f32[2,6,8,128]{3,2,1,0:T(8,128)} %get-tuple-element.27.links_ref), custom_call_target="tpu_custom_call" | custom-call | flops 8000000000 | bytes 6000000 | tf_op jit(solution)/shard_map/wave/pallas_call | solution.py:219
  176.2 21.5 %all_to_all.42 = bf16[8,200,384]{2,1,0:T(8,128)(2,1)} all-to-all(bf16[8,200,384]{2,1,0:T(8,128)(2,1)} %bitcast.40), channel_id=1, replica_groups=mesh['lat'=8,'wave'=4] {'lat'}, dimensions={0} | all-to-all | bytes 2457600 | tf_op jit(solution)/shard_map/all_to_all | solution.py:319
  197.8 7.8 %pair.5 = bf16[100,16,384]{2,1,0:T(8,128)(2,1)} custom-call(bf16[8,25,8,384]{3,2,1,0:T(8,128)(2,1)} %bitcast.44), custom_call_target="tpu_custom_call" | custom-call | flops 2000000000 | bytes 2400000 | tf_op jit(solution)/shard_map/pair/pallas_call | solution.py:239
  205.7 2.5 pad_maximum_fusion.2
  208.2 51.3 %all_to_all.43 = bf16[8,200,1184]{2,1,0:T(8,128)(2,1)} all-to-all(bf16[8,200,1184]{2,1,0:T(8,128)(2,1)S(1)} %pad_maximum_fusion.2), channel_id=1, replica_groups=mesh['lat'=8,'wave'=4] {'lat'}, dimensions={0} | all-to-all | bytes 7577600 | tf_op jit(solution)/shard_map/all_to_all | solution.py:315
  259.5 7.3 %wave.6 = bf16[2,800,384]{2,1,0:T(8,128)(2,1)} custom-call(bf16[2,800,1184]{2,1,0:T(8,128)(2,1)} %bitcast.37, f32[2,6,8,100]{3,2,1,0:T(8,128)} %get-tuple-element.30.factors_ref, f32[2,6,8,128]{3,2,1,0:T(8,128)} %get-tuple-element.26.links_ref), custom_call_target="tpu_custom_call" | custom-call | flops 8000000000 | bytes 6000000 | tf_op jit(solution)/shard_map/wave/pallas_call | solution.py:219
  266.9 21.5 %all_to_all.44 = bf16[8,200,384]{2,1,0:T(8,128)(2,1)} all-to-all(bf16[8,200,384]{2,1,0:T(8,128)(2,1)} %bitcast.41), channel_id=1, replica_groups=mesh['lat'=8,'wave'=4] {'lat'}, dimensions={0} | all-to-all | bytes 2457600 | tf_op jit(solution)/shard_map/all_to_all | solution.py:319
  288.4 7.9 %pair.6 = bf16[100,16,384]{2,1,0:T(8,128)(2,1)} custom-call(bf16[8,25,8,384]{3,2,1,0:T(8,128)(2,1)} %bitcast.45), custom_call_target="tpu_custom_call" | custom-call | flops 2000000000 | bytes 2400000 | tf_op jit(solution)/shard_map/pair/pallas_call | solution.py:239
  296.3 1.7 pad_maximum_fusion.3
  298.0 51.3 %all_to_all.45 = bf16[8,200,1184]{2,1,0:T(8,128)(2,1)} all-to-all(bf16[8,200,1184]{2,1,0:T(8,128)(2,1)S(1)} %pad_maximum_fusion.3), channel_id=1, replica_groups=mesh['lat'=8,'wave'=4] {'lat'}, dimensions={0} | all-to-all | bytes 7577600 | tf_op jit(solution)/shard_map/all_to_all | solution.py:315
  349.3 7.4 %wave.7 = bf16[2,800,384]{2,1,0:T(8,128)(2,1)} custom-call(bf16[2,800,1184]{2,1,0:T(8,128)(2,1)} %bitcast.35, f32[2,6,8,100]{3,2,1,0:T(8,128)} %get-tuple-element.29.factors_ref, f32[2,6,8,128]{3,2,1,0:T(8,128)} %get-tuple-element.25.links_ref), custom_call_target="tpu_custom_call" | custom-call | flops 8000000000 | bytes 6000000 | tf_op jit(solution)/shard_map/wave/pallas_call | solution.py:219
  356.7 21.5 %all_to_all.46 = bf16[8,200,384]{2,1,0:T(8,128)(2,1)} all-to-all(bf16[8,200,384]{2,1,0:T(8,128)(2,1)} %bitcast.42), channel_id=1, replica_groups=mesh['lat'=8,'wave'=4] {'lat'}, dimensions={0} | all-to-all | bytes 2457600 | tf_op jit(solution)/shard_map/all_to_all | solution.py:319
  378.2 7.8 %pair.7 = bf16[100,16,384]{2,1,0:T(8,128)(2,1)} custom-call(bf16[8,25,8,384]{3,2,1,0:T(8,128)(2,1)} %bitcast.46), custom_call_target="tpu_custom_call" | custom-call | flops 2000000000 | bytes 2400000 | tf_op jit(solution)/shard_map/pair/pallas_call | solution.py:239
  386.1 2.3 cosine_convert_fusion
  389.4 3.8 all-gather.13.cloned.1.call-done
  393.3 92.5 %all-gather.15.cloned.1.call-done = bf16[400,16,384]{2,1,0:T(8,128)(2,1)} async-done(((bf16[100,16,384]{2,1,0:T(8,128)(2,1)}), bf16[400,16,384]{2,1,0:T(8,128)(2,1)}) %all-gather.15.cloned.1.call-update) | async-done | bytes 4915216 | tf_op jit(solution)/shard_map/all_gather | solution.py:321
  485.8 36.3 %zonal.1 = bf16[800,38400]{1,0:T(8,128)(2,1)} custom-call(bf16[800,256]{1,0:T(8,128)(2,1)} %copy.20.trig_ref, bf16[4,100,16,384]{3,2,1,0:T(8,128)(2,1)} %bitcast.31, bf16[4,100,16,384]{3,2,1,0:T(8,128)(2,1)} %bitcast.32, bf16[4,100,16,384]{3,2,1,0:T(8,128)(2,1)} %bitcast.33, bf16[4,100,16,384]{3,2,1,0:T(8,128)(2,1)} %bitcast.34), custom_call_target="tpu_custom_call" | custom-call | flops 15728640000 | bytes 61440000 | tf_op jit(solution)/shard_map/zonal/pallas_call | solution.py:256
  (48 shorter events, 6.3 us)
Async XLA Ops:
  24.6 6.0 %copy-start.5 = (s32[128]{0:T(128)S(1)}, s32[128]{0:T(128)}, u32[]{:S(2)}) copy-start(s32[128]{0:T(128)} %param.8) | copy-start | bytes 1540
  24.6 6.8 %copy-start = (f32[32,1600]{1,0:T(8,128)S(1)}, f32[32,1600]{1,0:T(8,128)}, u32[]{:S(2)}) copy-start(f32[32,1600]{1,0:T(8,128)} %param.9) | copy-start | bytes 614404
  24.6 7.8 %copy-start.1 = (f32[32,1600]{1,0:T(8,128)S(1)}, f32[32,1600]{1,0:T(8,128)}, u32[]{:S(2)}) copy-start(f32[32,1600]{1,0:T(8,128)} %param.10) | copy-start | bytes 614404
  24.6 53.5 %all-to-all-start = ((bf16[8,200,1184]{2,1,0:T(8,128)(2,1)}), bf16[8,200,1184]{2,1,0:T(8,128)(2,1)}, u32[]{:S(2)}, u32[]{:S(2)}) async-start(bf16[8,200,1184]{2,1,0:T(8,128)(2,1)} %pad_maximum_fusion), calls=%async_computation | async-start | bytes 8192000 | tf_op jit(solution)/shard_map/all_to_all | solution.py:315
  29.9 359.5 %all-gather.9.cloned.1.call-start = ((), (), s32[]{:S(2)}) async-start(), calls=%async_computation.8 | async-start | bytes 6144000 | tf_op jit(solution)/shard_map/all_gather | solution.py:321
  30.7 0.6 copy-start.2
  35.6 0.7 copy-start.4
  115.0 274.5 %all-gather.11.cloned.1.call-start = ((), (), s32[]{:S(2)}) async-start(), calls=%async_computation.9 | async-start | bytes 6144000 | tf_op jit(solution)/shard_map/all_gather | solution.py:321
  205.6 187.6 %all-gather.13.cloned.1.call-start = ((), (), s32[]{:S(2)}) async-start(), calls=%async_computation.10 | async-start | bytes 6144000 | tf_op jit(solution)/shard_map/all_gather | solution.py:321
  296.3 189.5 %all-gather.15.cloned.1.call-start = ((), (), s32[]{:S(2)}) async-start(), calls=%async_computation.11 | async-start | bytes 6144000 | tf_op jit(solution)/shard_map/all_gather | solution.py:321
  378.2 7.9 %copy-start.3 = (s32[4,4,8]{2,1,0:T(4,128)S(1)}, s32[4,4,8]{2,1,0:T(4,128)}, u32[]{:S(2)}) copy-start(s32[4,4,8]{2,1,0:T(4,128)} %copy-done.2) | copy-start | bytes 1540
Sparse Core Ops, SparseCore 0:
  115.1 92.7 all-gather.8
  209.4 91.0 all-gather.10
  302.2 91.0 all-gather.12
  394.7 91.0 all-gather.14

commit v2 on v1

--- a/solution.py
+++ b/solution.py
@@ -17,11 +17,12 @@
 bf16 = jnp.bfloat16
 
 
-def zonal_matrix(wave_ids, lon_ids):
-    phase_index = lon_ids[:, None, None] * wave_ids[None] % NLON
+def zonal_matrix(blocks, lon_ids):
+    wave_ids = jnp.concatenate([jnp.concatenate([ids, ids]) for ids in blocks])
+    is_sine = jnp.concatenate([jnp.arange(2 * ids.size) >= ids.size for ids in blocks])
+    phase_index = lon_ids[:, None] * wave_ids[None, :] % NLON
     phase_angle = phase_index.astype(f32) * (2.0 * math.pi / NLON)
-    table = jnp.stack([jnp.cos(phase_angle), -jnp.sin(phase_angle)], axis=2).astype(bf16)
-    return table.reshape(lon_ids.shape[0], 2 * wave_ids.size)
+    return jnp.where(is_sine[None, :], -jnp.sin(phase_angle), jnp.cos(phase_angle)).astype(bf16)
 
 
 def factor_kernel(bands_ref, factors_ref, links_ref):
@@ -150,7 +151,7 @@
     home_ref[1] = (parts[0] - parts[1]).astype(bf16)
 
 
-def pair_kernel(rows_ref, pairs_ref):
+def pair_kernel(rows_ref, *pairs_refs):
     slots, groups, rows, width = rows_ref.shape
     order = slots * rows
     out_row = lax.broadcasted_iota(jnp.int32, (order, order), 0)
@@ -163,28 +164,24 @@
     def swap(values):
         return jnp.concatenate([values[:, width // 2 :], values[:, : width // 2]], axis=1)
 
-    def one(g, _):
+    for g in range(groups):
         block = rows_ref[:, g].astype(f32).reshape(order, width).astype(bf16)
         moved = jnp.dot(shuffle, block, preferred_element_type=f32)
         even_rows, odd_rows = moved[: order // 2], moved[order // 2 :]
         real = jnp.where(first_half, even_rows, swap(odd_rows)).reshape(rows // 2, slots, width)
         imag = jnp.where(first_half, swap(even_rows), odd_rows).reshape(rows // 2, slots, width)
-        pairs_ref[pl.ds(g * (rows // 2), rows // 2)] = jnp.concatenate([real, imag], axis=1).astype(bf16)
-        return 0
-
-    lax.fori_loop(0, groups, one, 0)
-
-
-def zonal_kernel(chunks, trig_ref, *refs):
+        both = jnp.concatenate([real, imag], axis=1).astype(bf16)
+        for n in range(rows // 2):
+            piece, place = divmod(g * (rows // 2) + n, pairs_refs[0].shape[0])
+            pairs_refs[piece][place] = both[n]
+
+
+def zonal_kernel(count, trig_ref, *refs):
     grid_ref = refs[-1]
-    waves, pairs, depth, width = refs[0].shape
+    pairs, _, width = refs[0].shape
     for r in range(0, pairs, 2):
         rhs = jnp.concatenate(
-            [
-                jnp.concatenate([refs[j][z, r + n] for j in range(chunks) for z in range(waves)], axis=0)
-                for n in range(2)
-            ],
-            axis=1,
+            [jnp.concatenate([refs[m][r + n] for m in range(count)], axis=0) for n in range(2)], axis=1
         )
         sums = jnp.dot(trig_ref[...], rhs, preferred_element_type=f32)
         grid_ref[:, r * width : (r + 2) * width] = sums.astype(bf16)
@@ -231,40 +228,60 @@
     )(arrived, factors, links)
 
 
-def pair_rows(rows):
+def pair_rows(rows, pieces=1):
     slots, count, width = rows.shape
     if count % 8 or slots % 8:
         split = rows.reshape(slots, count // 2, 2, 2, width // 2)
-        return split.transpose(1, 3, 0, 2, 4).reshape(count // 2, 2 * slots, width)
-    return pl.pallas_call(
+        joined = split.transpose(1, 3, 0, 2, 4).reshape(pieces, count // 2 // pieces, 2 * slots, width)
+        return [joined[n] for n in range(pieces)]
+    shape = jax.ShapeDtypeStruct((count // 2 // pieces, 2 * slots, width), bf16)
+    pairs = pl.pallas_call(
         pair_kernel,
-        out_shape=jax.ShapeDtypeStruct((count // 2, 2 * slots, width), bf16),
+        out_shape=[shape] * pieces,
         in_specs=whole_vmem(1),
-        out_specs=whole_vmem(1)[0],
+        out_specs=whole_vmem(pieces),
         compiler_params=params(),
         cost_estimate=pl.CostEstimate(flops=2_000_000_000, bytes_accessed=2_400_000, transcendentals=0),
         name="pair",
     )(rows.reshape(slots, count // 8, 8, width))
-
-
-def synthesize(trig, gathered):
+    return list(pairs)
+
+
+def synthesize(trig, whole, last):
     lons, depth = trig.shape
-    waves, pairs, rows, width = gathered[0].shape
-    step = next(n for n in (4, 2, 1) if pairs % n == 0)
-    assert step > 1
-    spec = pl.BlockSpec((waves, step, rows, width), lambda i: (0, i, 0, 0))
-    return pl.pallas_call(
-        functools.partial(zonal_kernel, len(gathered)),
-        out_shape=jax.ShapeDtypeStruct((lons, pairs * width), bf16),
-        grid=(pairs // step,),
-        in_specs=[pl.BlockSpec((lons, depth), lambda i: (0, 0))] + [spec] * len(gathered),
-        out_specs=pl.BlockSpec((lons, step * width), lambda i: (0, i)),
-        compiler_params=params(),
-        cost_estimate=pl.CostEstimate(
-            flops=2 * lons * depth * pairs * width, bytes_accessed=2 * lons * pairs * width, transcendentals=0
-        ),
-        name="zonal",
-    )(trig, *gathered)
+    pairs, _, width = whole[0].shape
+    piece_pairs = pairs // len(last)
+    step = next(n for n in (10, 8, 6, 4, 2) if piece_pairs % n == 0)
+    steps = piece_pairs // step
+    grid = None
+    for piece, extra in enumerate(last):
+
+        def spec(array, first):
+            return pl.BlockSpec((step,) + array.shape[1:], lambda i: (first + i, 0, 0))
+
+        first = piece * steps
+        operands = [trig, *whole, *extra]
+        in_specs = [pl.BlockSpec((lons, depth), lambda i: (0, 0))]
+        in_specs += [spec(array, first) for array in whole] + [spec(array, 0) for array in extra]
+        if grid is not None:
+            operands.append(grid)
+            in_specs.append(pl.BlockSpec(memory_space=pl.ANY))
+        grid = pl.pallas_call(
+            functools.partial(zonal_kernel, len(whole) + len(extra)),
+            out_shape=jax.ShapeDtypeStruct((lons, pairs * width), bf16),
+            grid=(steps,),
+            in_specs=in_specs,
+            out_specs=pl.BlockSpec((lons, step * width), lambda i, first=first: (0, first + i)),
+            input_output_aliases={len(operands) - 1: 0} if piece else {},
+            compiler_params=params(),
+            cost_estimate=pl.CostEstimate(
+                flops=2 * lons * depth * piece_pairs * width,
+                bytes_accessed=2 * lons * piece_pairs * width,
+                transcendentals=0,
+            ),
+            name="zonal",
+        )(*operands)
+    return grid
 
 
 def on_device(fourier_rows, legendre, wavenumber, lower_diag, main_diag, upper_diag):
@@ -305,25 +322,49 @@
     factors = factors.reshape(chunks, 2, 6, BLOCKS, steps)
     links = links.reshape(chunks, 2, 6, BLOCKS, 128)
 
-    gathered = []
-    ready = None
-    for j in range(chunks):
+    def outgoing(rows, table, j):
         pick = slice(j * lat_count, (j + 1) * lat_count)
-        outgoing = jnp.concatenate([fourier_rows[pick], legendre[pick].astype(bf16)], axis=2)
-        if ready is not None:
-            outgoing, _ = lax.optimization_barrier((outgoing, ready))
-        arrived = lax.all_to_all(outgoing, "lat", split_axis=0, concat_axis=0, tiled=True)
+        return jnp.concatenate([rows[pick], table[pick].astype(bf16)], axis=2)
+
+    def swap_lat(values):
+        return lax.all_to_all(values, "lat", split_axis=0, concat_axis=0, tiled=True)
+
+    def from_waves(values):
+        return [values] + [
+            lax.ppermute(values, "wave", [(w, (w + k) % wave_count) for w in range(wave_count)])
+            for k in range(1, wave_count)
+        ]
+
+    def wave_rows(arrived, j):
         arrived = arrived.reshape(2, pair_count, row_width + pair_count)
-        home = wave_step(arrived, factors[j], links[j], row_width)
-        home = home.reshape(lat_count, row_count, row_width)
-        rows = lax.all_to_all(home, "lat", split_axis=0, concat_axis=0, tiled=True)
-        ready = pair_rows(rows)
-        gathered.append(lax.all_gather(ready, "wave", axis=0))
+        return wave_step(arrived, factors[j], links[j], row_width).reshape(lat_count, row_count, row_width)
+
+    first_out = outgoing(fourier_rows, legendre, 0)
+    rows_later, table_later, _ = lax.optimization_barrier((fourier_rows, legendre, first_out))
+    ready = wave_rows(swap_lat(first_out), 0)
+    first_rows = from_waves(ready)
+    pieces = 2 if row_count % 8 == 0 else 1
+    whole, last = [], []
+    for j in range(1, chunks):
+        out, _ = lax.optimization_barrier((outgoing(rows_later, table_later, j), ready))
+        home = wave_rows(swap_lat(out), j)
+        pairs = pair_rows(swap_lat(home), pieces if j == chunks - 1 else 1)
+        ready = pairs[0]
+        parts = [from_waves(part) for part in pairs]
+        if j == chunks - 1:
+            last = parts
+        else:
+            whole += parts[0]
+    first_stack, _ = lax.optimization_barrier((jnp.stack(first_rows, axis=1), ready))
+    first_stack = swap_lat(first_stack).reshape(lat_count * wave_count, row_count, row_width)
+    whole = pair_rows(first_stack) + whole
 
     lon_dev = NLON // wave_count
     lon_ids = wave_pos * lon_dev + jnp.arange(lon_dev, dtype=jnp.int32)
-    trig = zonal_matrix(slot_ids.transpose(1, 0, 2).reshape(chunks * wave_count, lat_count), lon_ids)
-    return synthesize(trig, gathered)
+    sources = (wave_pos - jnp.arange(wave_count)) % wave_count
+    seen_ids = slot_ids[sources]
+    blocks = [seen_ids[:, 0].T.reshape(-1)] + [seen_ids[k, j] for j in range(1, chunks) for k in range(wave_count)]
+    return synthesize(zonal_matrix(blocks, lon_ids), whole, last)
 
 
 def solution(mesh):

time: 530 us -> 711 us (1.34); the launches traced: 529 us -> 701 us
  waiting for transfers between devices: 113 us -> 280 us
  starting transfers between devices: 5.46 us -> 161 us
  blocking collectives: 240 us -> 104 us
  Pallas kernels: 119 us -> 99.7 us
  other arithmetic: 21.4 us -> 35.6 us
  between operations: 13.3 us -> 0.81 us
    ppermute x0 -> x15, waiting for transfers between devices: none -> 210 us  [from_waves(): lax.ppermute(values, 'wave', [(w, (w + k) % wave_count) for w in range(wa...]
    all_to_all x7 -> x2, blocking collectives: 240 us -> 104 us  [swap_lat(): lax.all_to_all(values, 'lat', split_axis=0, concat_axis=0, tiled=True)]
    ppermute x0 -> x15, starting transfers between devices: none -> 133 us  [from_waves(): lax.ppermute(values, 'wave', [(w, (w + k) % wave_count) for w in range(wa...]
    all_gather x4 -> x0, waiting for transfers between devices: 96.4 us -> none  [on_device(): gathered.append(lax.all_gather(ready, 'wave', axis=0))]
    all_to_all x1 -> x6, waiting for transfers between devices: 17 us -> 69.5 us  [swap_lat(): lax.all_to_all(values, 'lat', split_axis=0, concat_axis=0, tiled=True)]
    all_to_all x1 -> x6, starting transfers between devices: 5.3 us -> 27.6 us  [swap_lat(): lax.all_to_all(values, 'lat', split_axis=0, concat_axis=0, tiled=True)]
    pallas_call x5 -> x6, Pallas kernels: 67.6 us -> 48.4 us  [the longest x2 33.1 us: synthesize(): pl.pallas_call(functools.partial(zonal_kernel, len(whole) + len(extra)),...]
    another operation x3 -> x2, other arithmetic: 10.6 us -> 17.5 us
  transfers between devices with their start and end apart: 5 -> 21, of which waited for: 3 -> 9; matrix products, arithmetic and copies ran while one was open for 3% -> 7% of each run, Pallas kernels for 13% -> 7%
where the time goes in v2:
time: 711 us; the launch traced here: 701 us
  waiting for transfers between devices  280 us (39%)
  starting transfers between devices  161 us (23%)
  blocking collectives  104 us (15%)
  Pallas kernels  99.7 us (14%)
  other arithmetic  35.6 us (5%)
  local copies, waits for them, and re-layouts  20.5 us (3%)
    ppermute x15, waiting for transfers between devices, from_waves(): lax.ppermute(values, 'wave', [(w, (w + k) % wave_count) for w in range(wa...  210 us
    ppermute x15, starting transfers between devices, from_waves(): lax.ppermute(values, 'wave', [(w, (w + k) % wave_count) for w in range(wa...  133 us
    all_to_all x2, blocking collectives, swap_lat(): lax.all_to_all(values, 'lat', split_axis=0, concat_axis=0, tiled=True)  104 us
    all_to_all x6, waiting for transfers between devices, swap_lat(): lax.all_to_all(values, 'lat', split_axis=0, concat_axis=0, tiled=True)  69.5 us
    pallas_call x2, Pallas kernels, synthesize(): pl.pallas_call(functools.partial(zonal_kernel, len(whole) + len(extra)),...  33.1 us
    pallas_call x4, Pallas kernels, wave_step(): pl.pallas_call(wave_kernel, out_shape=jax.ShapeDtypeStruct((2, pair_count...  29.7 us
    all_to_all x6, starting transfers between devices, swap_lat(): lax.all_to_all(values, 'lat', split_axis=0, concat_axis=0, tiled=True)  27.6 us
    pallas_call x1, Pallas kernels, make_factors(): pl.pallas_call(factor_kernel, out_shape=(jax.ShapeDtypeStruct((systems, 6...  21.7 us
  transfers between devices with their start and end apart: 21, of which 9 were waited for; matrix products, arithmetic and copies ran while one was open for 7% of the time, Pallas kernels for 7%

profile of v2, /device:TPU:0, one launch (start us, length us, event | category | flops | bytes accessed | tf_op | source)
XLA Modules:
  0.0 701.1 jit_solution(15033818061682535868)
XLA Ops:
  5.4 5.3 all-to-all-start
  12.3 13.1 %convert.9 = bf16[32,200,800]{2,1,0:T(8,128)(2,1)} convert(f32[32,200,800]{2,1,0:T(8,128)} %param.7) | non-fusion elementwise | flops 5120000 | bytes 30720000 | tf_op jit(solution)/shard_map/convert.2
  26.3 21.7 %factor.1 = (f32[8,6,8,100]{3,2,1,0:T(8,128)}, f32[8,6,8,128]{3,2,1,0:T(8,128)}) custom-call(f32[8,5,8,100]{3,2,1,0:T(8,128)} %copy-done.16), custom_call_target="tpu_custom_call" | custom-call | flops 2000000000 | bytes 2000000 | tf_op jit(solution)/shard_map/factor/pallas_call | solution.py:200
  52.9 5.2 fusion.11
  60.5 7.5 %wave.4 = bf16[2,800,384]{2,1,0:T(8,128)(2,1)} custom-call(bf16[2,800,1184]{2,1,0:T(8,128)(2,1)} %bitcast.15.arrived_ref, f32[2,6,8,100]{3,2,1,0:T(8,128)} %get-tuple-element.40.factors_ref, f32[2,6,8,128]{3,2,1,0:T(8,128)} %get-tuple-element.36.links_ref), custom_call_target="tpu_custom_call" | custom-call | flops 8000000000 | bytes 6000000 | tf_op jit(solution)/shard_map/wave/pallas_call | solution.py:216
  68.0 52.4 %all_to_all.40 = bf16[8,200,1184]{2,1,0:T(8,128)(2,1)} all-to-all(bf16[8,200,1184]{2,1,0:T(8,128)(2,1)S(1)} %copy-done), channel_id=1, replica_groups=mesh['lat'=8,'wave'=4] {'lat'}, dimensions={0} | all-to-all | bytes 7577600 | tf_op jit(solution)/shard_map/all_to_all | solution.py:330
  120.4 7.4 %wave.5 = bf16[2,800,384]{2,1,0:T(8,128)(2,1)} custom-call(bf16[2,800,1184]{2,1,0:T(8,128)(2,1)} %bitcast.65, f32[2,6,8,100]{3,2,1,0:T(8,128)} %get-tuple-element.39.factors_ref, f32[2,6,8,128]{3,2,1,0:T(8,128)} %get-tuple-element.35.links_ref), custom_call_target="tpu_custom_call" | custom-call | flops 8000000000 | bytes 6000000 | tf_op jit(solution)/shard_map/wave/pallas_call | solution.py:216
  127.8 4.3 all-to-all-start.2
  132.0 4.5 pad_maximum_fusion.3
  136.5 12.8 %all-to-all-done.2 = bf16[8,200,384]{2,1,0:T(8,128)(2,1)} async-done(((bf16[8,200,384]{2,1,0:T(8,128)(2,1)}), bf16[8,200,384]{2,1,0:T(8,128)(2,1)}, u32[]{:S(2)}, u32[]{:S(2)}) %all-to-all-start.2) | async-done | bytes 1228832 | tf_op jit(solution)/shard_map/all_to_all | solution.py:330
  152.4 51.5 %all_to_all.41 = bf16[8,200,1184]{2,1,0:T(8,128)(2,1)} all-to-all(bf16[8,200,1184]{2,1,0:T(8,128)(2,1)S(1)} %copy-done.1), channel_id=1, replica_groups=mesh['lat'=8,'wave'=4] {'lat'}, dimensions={0} | all-to-all | bytes 7577600 | tf_op jit(solution)/shard_map/all_to_all | solution.py:330
  203.9 7.4 %wave.6 = bf16[2,800,384]{2,1,0:T(8,128)(2,1)} custom-call(bf16[2,800,1184]{2,1,0:T(8,128)(2,1)} %bitcast.66, f32[2,6,8,100]{3,2,1,0:T(8,128)} %get-tuple-element.38.factors_ref, f32[2,6,8,128]{3,2,1,0:T(8,128)} %get-tuple-element.34.links_ref), custom_call_target="tpu_custom_call" | custom-call | flops 8000000000 | bytes 6000000 | tf_op jit(solution)/shard_map/wave/pallas_call | solution.py:216
  219.2 13.7 %all-to-all-done.4 = bf16[8,200,384]{2,1,0:T(8,128)(2,1)} async-done(((bf16[8,200,384]{2,1,0:T(8,128)(2,1)}), bf16[8,200,384]{2,1,0:T(8,128)(2,1)}, u32[]{:S(2)}, u32[]{:S(2)}) %all-to-all-start.4) | async-done | bytes 1228832 | tf_op jit(solution)/shard_map/all_to_all | solution.py:330
  235.8 4.7 all-to-all-start.5
  245.6 43.0 %all-to-all-done.5 = bf16[8,200,1184]{2,1,0:T(8,128)(2,1)} async-done(((bf16[8,200,1184]{2,1,0:T(8,128)(2,1)}), bf16[8,200,1184]{2,1,0:T(8,128)(2,1)}, u32[]{:S(2)}, u32[]{:S(2)}) %all-to-all-start.5) | async-done | bytes 3788832 | tf_op jit(solution)/shard_map/all_to_all | solution.py:330
  288.5 7.4 %wave.7 = bf16[2,800,384]{2,1,0:T(8,128)(2,1)} custom-call(bf16[2,800,1184]{2,1,0:T(8,128)(2,1)} %bitcast.30.arrived_ref, f32[2,6,8,100]{3,2,1,0:T(8,128)} %get-tuple-element.37.factors_ref, f32[2,6,8,128]{3,2,1,0:T(8,128)} %get-tuple-element.33.links_ref), custom_call_target="tpu_custom_call" | custom-call | flops 8000000000 | bytes 6000000 | tf_op jit(solution)/shard_map/wave/pallas_call | solution.py:216
  296.0 4.3 all-to-all-start.6
  300.2 50.1 %collective-permute-done.1 = bf16[8,200,384]{2,1,0:T(8,128)(2,1)} collective-permute-done((bf16[8,200,384]{2,1,0:T(8,128)(2,1)S(1)}, bf16[8,200,384]{2,1,0:T(8,128)(2,1)}, u32[]{:S(2)}, u32[]{:S(2)}) %collective-permute-start.1) | collective-permute-done | bytes 1228832 | tf_op jit(solution)/shard_map/ppermute | solution.py:334
  350.3 4.5 pad_maximum_fusion
  357.6 4.9 all-to-all-start.7
  369.2 23.2 %collective-permute-done.5.refs_4_ = bf16[100,16,384]{2,1,0:T(8,128)(2,1)S(1)} collective-permute-done((bf16[100,16,384]{2,1,0:T(8,128)(2,1)S(1)}, bf16[100,16,384]{2,1,0:T(8,128)(2,1)S(1)}, u32[]{:S(2)}, u32[]{:S(2)}) %collective-permute-start.5) | collective-permute-done | bytes 1228832 | tf_op jit(solution)/shard_map/ppermute | solution.py:334
  395.5 76.7 %collective-permute-done.4.refs_3_ = bf16[100,16,384]{2,1,0:T(8,128)(2,1)} collective-permute-done((bf16[100,16,384]{2,1,0:T(8,128)(2,1)S(1)}, bf16[100,16,384]{2,1,0:T(8,128)(2,1)}, u32[]{:S(2)}, u32[]{:S(2)}) %collective-permute-start.4) | collective-permute-done | bytes 1228832 | tf_op jit(solution)/shard_map/ppermute | solution.py:334
  472.2 53.0 %collective-permute-start.13 = (bf16[50,16,384]{2,1,0:T(8,128)(2,1)S(1)}, bf16[50,16,384]{2,1,0:T(8,128)(2,1)S(1)}, u32[]{:S(2)}, u32[]{:S(2)}) collective-permute-start(bf16[50,16,384]{2,1,0:T(8,128)(2,1)S(1)} %copy-done.7), channel_id=1, source_target_pairs={{0,2},{1,3},{2,0},{3,1},{4,6},{5,7},{6,4},{7,5},{8,10},{9,11},{10,... | collective-permute-start | bytes 1843208 | tf_op jit(solution)/shard_map/ppermute | solution.py:334
  525.2 52.9 %collective-permute-start.12 = (bf16[50,16,384]{2,1,0:T(8,128)(2,1)S(1)}, bf16[50,16,384]{2,1,0:T(8,128)(2,1)S(1)}, u32[]{:S(2)}, u32[]{:S(2)}) collective-permute-start(bf16[50,16,384]{2,1,0:T(8,128)(2,1)S(1)} %copy-done.7), channel_id=1, source_target_pairs={{0,1},{1,2},{2,3},{3,0},{4,5},{5,6},{6,7},{7,4},{8,9},{9,10},{10,1... | collective-permute-start | bytes 1843208 | tf_op jit(solution)/shard_map/ppermute | solution.py:334
  578.3 4.8 select_convert_fusion.trig_ref
  583.1 6.6 pair.7.refs_0_
  589.8 14.1 %collective-permute-done.7.refs_7_ = bf16[100,16,384]{2,1,0:T(8,128)(2,1)} collective-permute-done((bf16[100,16,384]{2,1,0:T(8,128)(2,1)S(1)}, bf16[100,16,384]{2,1,0:T(8,128)(2,1)}, u32[]{:S(2)}, u32[]{:S(2)}) %collective-permute-start.7) | collective-permute-done | bytes 1228832 | tf_op jit(solution)/shard_map/ppermute | solution.py:334
  603.9 14.0 %collective-permute-start.9 = (bf16[50,16,384]{2,1,0:T(8,128)(2,1)S(1)}, bf16[50,16,384]{2,1,0:T(8,128)(2,1)S(1)}, u32[]{:S(2)}, u32[]{:S(2)}) collective-permute-start(bf16[50,16,384]{2,1,0:T(8,128)(2,1)S(1)} %copy-done.6), channel_id=1, source_target_pairs={{0,1},{1,2},{2,3},{3,0},{4,5},{5,6},{6,7},{7,4},{8,9},{9,10},{10,1... | collective-permute-start | bytes 1843208 | tf_op jit(solution)/shard_map/ppermute | solution.py:334
  617.9 38.5 %collective-permute-done.13.refs_11_ = bf16[50,16,384]{2,1,0:T(8,128)(2,1)S(1)} collective-permute-done((bf16[50,16,384]{2,1,0:T(8,128)(2,1)S(1)}, bf16[50,16,384]{2,1,0:T(8,128)(2,1)S(1)}, u32[]{:S(2)}, u32[]{:S(2)}) %collective-permute-start.13) | collective-permute-done | bytes 614432 | tf_op jit(solution)/shard_map/ppermute | solution.py:334
  658.0 16.5 %zonal.2.refs_13_ = bf16[800,38400]{1,0:T(8,128)(2,1)} custom-call(bf16[800,256]{1,0:T(8,128)(2,1)} %select_convert_fusion.trig_ref, bf16[100,64,384]{2,1,0:T(8,128)(2,1)} %pair.7.refs_0_, bf16[100,16,384]{2,1,0:T(8,128)(2,1)} %pair.4.refs_1_, bf16[100,16,384]{2,1,0:T(8,128)(2,1)} %collective-permute-done.3.refs_2_, ...), custom_call_target="tpu_custom_call" | custom-call | flops 7864320000 | bytes 30720000 | tf_op jit(solution)/shard_map/zonal/pallas_call | solution.py:269
  674.6 7.8 %collective-permute-done.10.refs_11_ = bf16[50,16,384]{2,1,0:T(8,128)(2,1)S(1)} collective-permute-done((bf16[50,16,384]{2,1,0:T(8,128)(2,1)S(1)}, bf16[50,16,384]{2,1,0:T(8,128)(2,1)S(1)}, u32[]{:S(2)}, u32[]{:S(2)}) %collective-permute-start.10) | collective-permute-done | bytes 614432 | tf_op jit(solution)/shard_map/ppermute | solution.py:334
  684.1 16.6 %zonal.3 = bf16[800,38400]{1,0:T(8,128)(2,1)} custom-call(bf16[800,256]{1,0:T(8,128)(2,1)} %select_convert_fusion.trig_ref, bf16[100,64,384]{2,1,0:T(8,128)(2,1)} %pair.7.refs_0_, bf16[100,16,384]{2,1,0:T(8,128)(2,1)} %pair.4.refs_1_, bf16[100,16,384]{2,1,0:T(8,128)(2,1)} %collective-permute-done.3.refs_2_, ...), custom_call_target="tpu_custom_call", output_to_operand_aliasing={{}: (14, {})} | custom-call | flops 7864320000 | bytes 30720000 | tf_op jit(solution)/shard_map/zonal/pallas_call | solution.py:269
  (113 shorter events, 50.2 us)
Async XLA Ops:
  5.4 5.4 copy-start.17
  5.4 5.9 copy-start.13
  5.4 6.2 copy-start.14
  5.4 6.5 copy-start.15
  5.4 55.1 %all-to-all-start = ((bf16[8,200,1184]{2,1,0:T(8,128)(2,1)}), bf16[8,200,1184]{2,1,0:T(8,128)(2,1)}, u32[]{:S(2)}, u32[]{:S(2)}) async-start(bf16[8,200,1184]{2,1,0:T(8,128)(2,1)} %pad_maximum_fusion.1), calls=%async_computation | async-start | bytes 8192000 | tf_op jit(solution)/shard_map/all_to_all | solution.py:330
  11.6 39.4 %slice-start = ((s8[4915200]{0:T(1024)(128)(4,1)}), s8[720896]{0:T(1024)(128)(4,1)S(1)}, s32[]{:S(2)}) async-start(s8[4915200]{0:T(1024)(128)(4,1)} %bitcast.63), calls=%async_computation.8 | async-start | bytes 1441792
  12.3 38.8 %slice-start.1 = ((s8[4915200]{0:T(1024)(128)(4,1)}), s8[4194304]{0:T(1024)(128)(4,1)S(1)}, s32[]{:S(2)}) async-start(s8[4915200]{0:T(1024)(128)(4,1)} %bitcast.63), calls=%async_computation.9 | async-start | bytes 8388608
  60.5 7.5 %copy-start = (bf16[8,200,1184]{2,1,0:T(8,128)(2,1)S(1)}, bf16[8,200,1184]{2,1,0:T(8,128)(2,1)}, u32[]{:S(2)}) copy-start(bf16[8,200,1184]{2,1,0:T(8,128)(2,1)} %pad_maximum_fusion.4) | copy-start | bytes 11366404
  127.8 21.6 %all-to-all-start.2 = ((bf16[8,200,384]{2,1,0:T(8,128)(2,1)}), bf16[8,200,384]{2,1,0:T(8,128)(2,1)}, u32[]{:S(2)}, u32[]{:S(2)}) async-start(bf16[8,200,384]{2,1,0:T(8,128)(2,1)} %bitcast.74), calls=%async_computation.2 | async-start | bytes 2457600 | tf_op jit(solution)/shard_map/all_to_all | solution.py:330
  211.2 21.6 %all-to-all-start.4 = ((bf16[8,200,384]{2,1,0:T(8,128)(2,1)}), bf16[8,200,384]{2,1,0:T(8,128)(2,1)}, u32[]{:S(2)}, u32[]{:S(2)}) async-start(bf16[8,200,384]{2,1,0:T(8,128)(2,1)} %bitcast.73), calls=%async_computation.4 | async-start | bytes 2457600 | tf_op jit(solution)/shard_map/all_to_all | solution.py:330
  235.8 52.8 %all-to-all-start.5 = ((bf16[8,200,1184]{2,1,0:T(8,128)(2,1)}), bf16[8,200,1184]{2,1,0:T(8,128)(2,1)}, u32[]{:S(2)}, u32[]{:S(2)}) async-start(bf16[8,200,1184]{2,1,0:T(8,128)(2,1)} %pad_maximum_fusion.2), calls=%async_computation.5 | async-start | bytes 8192000 | tf_op jit(solution)/shard_map/all_to_all | solution.py:330
  240.5 59.7 %collective-permute-start.2 = (bf16[8,200,384]{2,1,0:T(8,128)(2,1)S(1)}, bf16[8,200,384]{2,1,0:T(8,128)(2,1)S(1)}, u32[]{:S(2)}, u32[]{:S(2)}) collective-permute-start(bf16[8,200,384]{2,1,0:T(8,128)(2,1)S(1)} %bitcast.67), channel_id=1, source_target_pairs={{0,3},{1,0},{2,1},{3,2},{4,7},{5,4},{6,5},{7,6},{8,11},{9,8},{10,9... | collective-permute-start | bytes 3686408 | tf_op jit(solution)/shard_map/ppermute | solution.py:334
  244.6 105.8 %collective-permute-start.1 = (bf16[8,200,384]{2,1,0:T(8,128)(2,1)S(1)}, bf16[8,200,384]{2,1,0:T(8,128)(2,1)}, u32[]{:S(2)}, u32[]{:S(2)}) collective-permute-start(bf16[8,200,384]{2,1,0:T(8,128)(2,1)S(1)} %bitcast.68), channel_id=1, source_target_pairs={{0,2},{1,3},{2,0},{3,1},{4,6},{5,7},{6,4},{7,5},{8,10},{9,11},{10,... | collective-permute-start | bytes 3686408 | tf_op jit(solution)/shard_map/ppermute | solution.py:334
  244.6 105.8 %collective-permute-start = (bf16[8,200,384]{2,1,0:T(8,128)(2,1)S(1)}, bf16[8,200,384]{2,1,0:T(8,128)(2,1)}, u32[]{:S(2)}, u32[]{:S(2)}) collective-permute-start(bf16[8,200,384]{2,1,0:T(8,128)(2,1)S(1)} %bitcast.69), channel_id=1, source_target_pairs={{0,1},{1,2},{2,3},{3,0},{4,5},{5,6},{6,7},{7,4},{8,9},{9,10},{10,1... | collective-permute-start | bytes 3686408 | tf_op jit(solution)/shard_map/ppermute | solution.py:334
  296.0 58.9 %all-to-all-start.6 = ((bf16[8,200,384]{2,1,0:T(8,128)(2,1)}), bf16[8,200,384]{2,1,0:T(8,128)(2,1)}, u32[]{:S(2)}, u32[]{:S(2)}) async-start(bf16[8,200,384]{2,1,0:T(8,128)(2,1)} %bitcast.72), calls=%async_computation.6 | async-start | bytes 2457600 | tf_op jit(solution)/shard_map/all_to_all | solution.py:330
  357.6 9.8 %copy-start.3 = (bf16[100,16,384]{2,1,0:T(8,128)(2,1)S(1)}, bf16[100,16,384]{2,1,0:T(8,128)(2,1)}, u32[]{:S(2)}) copy-start(bf16[100,16,384]{2,1,0:T(8,128)(2,1)} %pair.5.refs_5_) | copy-start | bytes 3686404
  357.6 114.6 %copy-start.7 = (bf16[50,16,384]{2,1,0:T(8,128)(2,1)S(1)}, bf16[50,16,384]{2,1,0:T(8,128)(2,1)}, u32[]{:S(2)}) copy-start(bf16[50,16,384]{2,1,0:T(8,128)(2,1)} %get-tuple-element.22.refs_9_) | copy-start | bytes 1843204
  357.6 225.6 %all-to-all-start.7 = ((bf16[8,4,200,384]{3,2,1,0:T(8,128)(2,1)}), bf16[8,4,200,384]{3,2,1,0:T(8,128)(2,1)}, u32[]{:S(2)}, u32[]{:S(2)}) async-start(bf16[8,4,200,384]{3,2,1,0:T(8,128)(2,1)} %pad_maximum_fusion), calls=%async_computation.7 | async-start | bytes 9830400 | tf_op jit(solution)/shard_map/all_to_all | solution.py:330
  362.4 29.9 %collective-permute-start.5 = (bf16[100,16,384]{2,1,0:T(8,128)(2,1)S(1)}, bf16[100,16,384]{2,1,0:T(8,128)(2,1)S(1)}, u32[]{:S(2)}, u32[]{:S(2)}) collective-permute-start(bf16[100,16,384]{2,1,0:T(8,128)(2,1)S(1)} %copy-done.2), channel_id=1, source_target_pairs={{0,3},{1,0},{2,1},{3,2},{4,7},{5,4},{6,5},{7,6},{8,11},{9,8},{10,9... | collective-permute-start | bytes 3686408 | tf_op jit(solution)/shard_map/ppermute | solution.py:334
  362.5 109.7 %collective-permute-start.4 = (bf16[100,16,384]{2,1,0:T(8,128)(2,1)S(1)}, bf16[100,16,384]{2,1,0:T(8,128)(2,1)}, u32[]{:S(2)}, u32[]{:S(2)}) collective-permute-start(bf16[100,16,384]{2,1,0:T(8,128)(2,1)S(1)} %copy-done.2), channel_id=1, source_target_pairs={{0,2},{1,3},{2,0},{3,1},{4,6},{5,7},{6,4},{7,5},{8,10},{9,11},{10,... | collective-permute-start | bytes 3686408 | tf_op jit(solution)/shard_map/ppermute | solution.py:334
  365.4 106.8 %collective-permute-start.3 = (bf16[100,16,384]{2,1,0:T(8,128)(2,1)S(1)}, bf16[100,16,384]{2,1,0:T(8,128)(2,1)}, u32[]{:S(2)}, u32[]{:S(2)}) collective-permute-start(bf16[100,16,384]{2,1,0:T(8,128)(2,1)S(1)} %copy-done.2), channel_id=1, source_target_pairs={{0,1},{1,2},{2,3},{3,0},{4,5},{5,6},{6,7},{7,4},{8,9},{9,10},{10,1... | collective-permute-start | bytes 3686408 | tf_op jit(solution)/shard_map/ppermute | solution.py:334
  367.3 157.9 %collective-permute-start.8 = (bf16[100,16,384]{2,1,0:T(8,128)(2,1)S(1)}, bf16[100,16,384]{2,1,0:T(8,128)(2,1)}, u32[]{:S(2)}, u32[]{:S(2)}) collective-permute-start(bf16[100,16,384]{2,1,0:T(8,128)(2,1)S(1)} %copy-done.3), channel_id=1, source_target_pairs={{0,3},{1,0},{2,1},{3,2},{4,7},{5,4},{6,5},{7,6},{8,11},{9,8},{10,9... | collective-permute-start | bytes 3686408 | tf_op jit(solution)/shard_map/ppermute | solution.py:334
  369.2 234.7 %collective-permute-start.7 = (bf16[100,16,384]{2,1,0:T(8,128)(2,1)S(1)}, bf16[100,16,384]{2,1,0:T(8,128)(2,1)}, u32[]{:S(2)}, u32[]{:S(2)}) collective-permute-start(bf16[100,16,384]{2,1,0:T(8,128)(2,1)S(1)} %copy-done.3), channel_id=1, source_target_pairs={{0,2},{1,3},{2,0},{3,1},{4,6},{5,7},{6,4},{7,5},{8,10},{9,11},{10,... | collective-permute-start | bytes 3686408 | tf_op jit(solution)/shard_map/ppermute | solution.py:334
  393.4 210.5 %collective-permute-start.6 = (bf16[100,16,384]{2,1,0:T(8,128)(2,1)S(1)}, bf16[100,16,384]{2,1,0:T(8,128)(2,1)}, u32[]{:S(2)}, u32[]{:S(2)}) collective-permute-start(bf16[100,16,384]{2,1,0:T(8,128)(2,1)S(1)} %copy-done.3), channel_id=1, source_target_pairs={{0,1},{1,2},{2,3},{3,0},{4,5},{5,6},{6,7},{7,4},{8,9},{9,10},{10,1... | collective-permute-start | bytes 3686408 | tf_op jit(solution)/shard_map/ppermute | solution.py:334
  472.2 131.8 %collective-permute-start.14 = (bf16[50,16,384]{2,1,0:T(8,128)(2,1)S(1)}, bf16[50,16,384]{2,1,0:T(8,128)(2,1)}, u32[]{:S(2)}, u32[]{:S(2)}) collective-permute-start(bf16[50,16,384]{2,1,0:T(8,128)(2,1)S(1)} %copy-done.7), channel_id=1, source_target_pairs={{0,3},{1,0},{2,1},{3,2},{4,7},{5,4},{6,5},{7,6},{8,11},{9,8},{10,9... | collective-permute-start | bytes 1843208 | tf_op jit(solution)/shard_map/ppermute | solution.py:334
  472.2 184.2 %collective-permute-start.13 = (bf16[50,16,384]{2,1,0:T(8,128)(2,1)S(1)}, bf16[50,16,384]{2,1,0:T(8,128)(2,1)S(1)}, u32[]{:S(2)}, u32[]{:S(2)}) collective-permute-start(bf16[50,16,384]{2,1,0:T(8,128)(2,1)S(1)} %copy-done.7), channel_id=1, source_target_pairs={{0,2},{1,3},{2,0},{3,1},{4,6},{5,7},{6,4},{7,5},{8,10},{9,11},{10,... | collective-permute-start | bytes 1843208 | tf_op jit(solution)/shard_map/ppermute | solution.py:334
  525.2 131.2 %collective-permute-start.12 = (bf16[50,16,384]{2,1,0:T(8,128)(2,1)S(1)}, bf16[50,16,384]{2,1,0:T(8,128)(2,1)S(1)}, u32[]{:S(2)}, u32[]{:S(2)}) collective-permute-start(bf16[50,16,384]{2,1,0:T(8,128)(2,1)S(1)} %copy-done.7), channel_id=1, source_target_pairs={{0,1},{1,2},{2,3},{3,0},{4,5},{5,6},{6,7},{7,4},{8,9},{9,10},{10,1... | collective-permute-start | bytes 1843208 | tf_op jit(solution)/shard_map/ppermute | solution.py:334
  583.1 20.7 %copy-start.6 = (bf16[50,16,384]{2,1,0:T(8,128)(2,1)S(1)}, bf16[50,16,384]{2,1,0:T(8,128)(2,1)}, u32[]{:S(2)}) copy-start(bf16[50,16,384]{2,1,0:T(8,128)(2,1)} %get-tuple-element.24.refs_9_) | copy-start | bytes 1843204
  603.8 70.8 %collective-permute-start.11 = (bf16[50,16,384]{2,1,0:T(8,128)(2,1)S(1)}, bf16[50,16,384]{2,1,0:T(8,128)(2,1)S(1)}, u32[]{:S(2)}, u32[]{:S(2)}) collective-permute-start(bf16[50,16,384]{2,1,0:T(8,128)(2,1)S(1)} %copy-done.6), channel_id=1, source_target_pairs={{0,3},{1,0},{2,1},{3,2},{4,7},{5,4},{6,5},{7,6},{8,11},{9,8},{10,9... | collective-permute-start | bytes 1843208 | tf_op jit(solution)/shard_map/ppermute | solution.py:334
  603.8 78.6 %collective-permute-start.10 = (bf16[50,16,384]{2,1,0:T(8,128)(2,1)S(1)}, bf16[50,16,384]{2,1,0:T(8,128)(2,1)S(1)}, u32[]{:S(2)}, u32[]{:S(2)}) collective-permute-start(bf16[50,16,384]{2,1,0:T(8,128)(2,1)S(1)} %copy-done.6), channel_id=1, source_target_pairs={{0,2},{1,3},{2,0},{3,1},{4,6},{5,7},{6,4},{7,5},{8,10},{9,11},{10,... | collective-permute-start | bytes 1843208 | tf_op jit(solution)/shard_map/ppermute | solution.py:334
  603.9 78.5 %collective-permute-start.9 = (bf16[50,16,384]{2,1,0:T(8,128)(2,1)S(1)}, bf16[50,16,384]{2,1,0:T(8,128)(2,1)S(1)}, u32[]{:S(2)}, u32[]{:S(2)}) collective-permute-start(bf16[50,16,384]{2,1,0:T(8,128)(2,1)S(1)} %copy-done.6), channel_id=1, source_target_pairs={{0,1},{1,2},{2,3},{3,0},{4,5},{5,6},{6,7},{7,4},{8,9},{9,10},{10,1... | collective-permute-start | bytes 1843208 | tf_op jit(solution)/shard_map/ppermute | solution.py:334
  674.6 7.8 %copy-start.10 = (bf16[50,16,384]{2,1,0:T(8,128)(2,1)}, bf16[50,16,384]{2,1,0:T(8,128)(2,1)S(1)}, u32[]{:S(2)}) copy-start(bf16[50,16,384]{2,1,0:T(8,128)(2,1)S(1)} %collective-permute-done.11.refs_12_) | copy-start | bytes 1843204
  (10 other events, 20.6 us)

commit v3 on v2

--- a/solution.py
+++ b/solution.py
@@ -164,6 +164,7 @@
     def swap(values):
         return jnp.concatenate([values[:, width // 2 :], values[:, : width // 2]], axis=1)
 
+    places = [ref.at[n] for ref in pairs_refs for n in range(ref.shape[0])]
     for g in range(groups):
         block = rows_ref[:, g].astype(f32).reshape(order, width).astype(bf16)
         moved = jnp.dot(shuffle, block, preferred_element_type=f32)
@@ -172,19 +173,27 @@
         imag = jnp.where(first_half, swap(even_rows), odd_rows).reshape(rows // 2, slots, width)
         both = jnp.concatenate([real, imag], axis=1).astype(bf16)
         for n in range(rows // 2):
-            piece, place = divmod(g * (rows // 2) + n, pairs_refs[0].shape[0])
-            pairs_refs[piece][place] = both[n]
-
-
-def zonal_kernel(count, trig_ref, *refs):
+            places[g * (rows // 2) + n][...] = both[n]
+
+
+def zonal_kernel(trig_ref, *refs):
     grid_ref = refs[-1]
-    pairs, _, width = refs[0].shape
+    pairs, width = refs[0].shape[-3], refs[0].shape[-1]
+
+    def coefficients(r):
+        found = []
+        for ref in refs[:-1]:
+            found += [ref[r]] if ref.ndim == 3 else [ref[z, r] for z in range(ref.shape[0])]
+        return jnp.concatenate(found, axis=0)
+
     for r in range(0, pairs, 2):
-        rhs = jnp.concatenate(
-            [jnp.concatenate([refs[m][r + n] for m in range(count)], axis=0) for n in range(2)], axis=1
-        )
+        rhs = jnp.concatenate([coefficients(r), coefficients(r + 1)], axis=1)
         sums = jnp.dot(trig_ref[...], rhs, preferred_element_type=f32)
         grid_ref[:, r * width : (r + 2) * width] = sums.astype(bf16)
+
+
+def zonal_tail_kernel(trig_ref, *refs):
+    zonal_kernel(trig_ref, *refs[:-2], refs[-1])
 
 
 def params():
@@ -228,18 +237,22 @@
     )(arrived, factors, links)
 
 
-def pair_rows(rows, pieces=1):
+def cut_pairs(count):
+    pairs = count // 2
+    return [pairs * 4 // 5, pairs // 5] if pairs % 10 == 0 and count % 8 == 0 else [pairs]
+
+
+def pair_rows(rows, pieces):
     slots, count, width = rows.shape
     if count % 8 or slots % 8:
         split = rows.reshape(slots, count // 2, 2, 2, width // 2)
-        joined = split.transpose(1, 3, 0, 2, 4).reshape(pieces, count // 2 // pieces, 2 * slots, width)
-        return [joined[n] for n in range(pieces)]
-    shape = jax.ShapeDtypeStruct((count // 2 // pieces, 2 * slots, width), bf16)
+        joined = split.transpose(1, 3, 0, 2, 4).reshape(count // 2, 2 * slots, width)
+        return [joined[sum(pieces[:n]) : sum(pieces[: n + 1])] for n in range(len(pieces))]
     pairs = pl.pallas_call(
         pair_kernel,
-        out_shape=[shape] * pieces,
+        out_shape=[jax.ShapeDtypeStruct((piece, 2 * slots, width), bf16) for piece in pieces],
         in_specs=whole_vmem(1),
-        out_specs=whole_vmem(pieces),
+        out_specs=whole_vmem(len(pieces)),
         compiler_params=params(),
         cost_estimate=pl.CostEstimate(flops=2_000_000_000, bytes_accessed=2_400_000, transcendentals=0),
         name="pair",
@@ -247,41 +260,37 @@
     return list(pairs)
 
 
-def synthesize(trig, whole, last):
+def synthesize(trig, whole, extra, first, pieces, grid):
     lons, depth = trig.shape
-    pairs, _, width = whole[0].shape
-    piece_pairs = pairs // len(last)
-    step = next(n for n in (10, 8, 6, 4, 2) if piece_pairs % n == 0)
-    steps = piece_pairs // step
-    grid = None
-    for piece, extra in enumerate(last):
-
-        def spec(array, first):
-            return pl.BlockSpec((step,) + array.shape[1:], lambda i: (first + i, 0, 0))
-
-        first = piece * steps
-        operands = [trig, *whole, *extra]
-        in_specs = [pl.BlockSpec((lons, depth), lambda i: (0, 0))]
-        in_specs += [spec(array, first) for array in whole] + [spec(array, 0) for array in extra]
-        if grid is not None:
-            operands.append(grid)
-            in_specs.append(pl.BlockSpec(memory_space=pl.ANY))
-        grid = pl.pallas_call(
-            functools.partial(zonal_kernel, len(whole) + len(extra)),
-            out_shape=jax.ShapeDtypeStruct((lons, pairs * width), bf16),
-            grid=(steps,),
-            in_specs=in_specs,
-            out_specs=pl.BlockSpec((lons, step * width), lambda i, first=first: (0, first + i)),
-            input_output_aliases={len(operands) - 1: 0} if piece else {},
-            compiler_params=params(),
-            cost_estimate=pl.CostEstimate(
-                flops=2 * lons * depth * piece_pairs * width,
-                bytes_accessed=2 * lons * piece_pairs * width,
-                transcendentals=0,
-            ),
-            name="zonal",
-        )(*operands)
-    return grid
+    piece, pairs = extra[0].shape[-3], sum(pieces)
+    width = extra[0].shape[-1]
+    step = next(n for n in (10, 8, 6, 4, 2) if piece % n == 0 and first % n == 0)
+    ahead = first // step
+
+    def spec(array, shift):
+        lead = array.shape[:-3]
+        block = lead + (step,) + array.shape[-2:]
+        return pl.BlockSpec(block, lambda i: (0,) * len(lead) + (shift + i, 0, 0))
+
+    operands = [trig, *whole, *extra]
+    in_specs = [pl.BlockSpec((lons, depth), lambda i: (0, 0))]
+    in_specs += [spec(array, ahead) for array in whole] + [spec(array, 0) for array in extra]
+    if grid is not None:
+        operands.append(grid)
+        in_specs.append(pl.BlockSpec(memory_space=pl.ANY))
+    return pl.pallas_call(
+        zonal_kernel if grid is None else zonal_tail_kernel,
+        out_shape=jax.ShapeDtypeStruct((lons, pairs * width), bf16),
+        grid=(piece // step,),
+        in_specs=in_specs,
+        out_specs=pl.BlockSpec((lons, step * width), lambda i: (0, ahead + i)),
+        input_output_aliases={} if grid is None else {len(operands) - 1: 0},
+        compiler_params=params(),
+        cost_estimate=pl.CostEstimate(
+            flops=4 * lons * depth * piece * width, bytes_accessed=2 * lons * piece * width, transcendentals=0
+        ),
+        name="zonal",
+    )(*operands)
 
 
 def on_device(fourier_rows, legendre, wavenumber, lower_diag, main_diag, upper_diag):
@@ -329,6 +338,9 @@
     def swap_lat(values):
         return lax.all_to_all(values, "lat", split_axis=0, concat_axis=0, tiled=True)
 
+    def gather_waves(values):
+        return lax.all_gather(values, "wave", axis=0)
+
     def from_waves(values):
         return [values] + [
             lax.ppermute(values, "wave", [(w, (w + k) % wave_count) for w in range(wave_count)])
@@ -342,29 +354,35 @@
     first_out = outgoing(fourier_rows, legendre, 0)
     rows_later, table_later, _ = lax.optimization_barrier((fourier_rows, legendre, first_out))
     ready = wave_rows(swap_lat(first_out), 0)
-    first_rows = from_waves(ready)
-    pieces = 2 if row_count % 8 == 0 else 1
+    first_rows = gather_waves(ready)
+    pieces = cut_pairs(row_count)
     whole, last = [], []
     for j in range(1, chunks):
         out, _ = lax.optimization_barrier((outgoing(rows_later, table_later, j), ready))
         home = wave_rows(swap_lat(out), j)
-        pairs = pair_rows(swap_lat(home), pieces if j == chunks - 1 else 1)
+        pairs = pair_rows(swap_lat(home), pieces if j == chunks - 1 else [row_count // 2])
         ready = pairs[0]
-        parts = [from_waves(part) for part in pairs]
         if j == chunks - 1:
-            last = parts
+            last = pairs
         else:
-            whole += parts[0]
-    first_stack, _ = lax.optimization_barrier((jnp.stack(first_rows, axis=1), ready))
+            whole.append(gather_waves(ready))
+    last_gathered = gather_waves(last[0])
+    first_stack, _ = lax.optimization_barrier((first_rows.swapaxes(0, 1), ready))
     first_stack = swap_lat(first_stack).reshape(lat_count * wave_count, row_count, row_width)
-    whole = pair_rows(first_stack) + whole
+    whole = pair_rows(first_stack, [row_count // 2]) + whole
 
     lon_dev = NLON // wave_count
     lon_ids = wave_pos * lon_dev + jnp.arange(lon_dev, dtype=jnp.int32)
-    sources = (wave_pos - jnp.arange(wave_count)) % wave_count
-    seen_ids = slot_ids[sources]
-    blocks = [seen_ids[:, 0].T.reshape(-1)] + [seen_ids[k, j] for j in range(1, chunks) for k in range(wave_count)]
-    return synthesize(zonal_matrix(blocks, lon_ids), whole, last)
+    blocks = [slot_ids[:, 0].T.reshape(-1)]
+    blocks += [slot_ids[w, j] for j in range(1, chunks) for w in range(wave_count)]
+    grid = synthesize(zonal_matrix(blocks, lon_ids), whole, [last_gathered], 0, pieces, None)
+    if len(pieces) > 1:
+        rest, _, _ = lax.optimization_barrier((last[1], last_gathered, whole[0]))
+        sources = (wave_pos - jnp.arange(wave_count)) % wave_count
+        seen_ids = slot_ids[sources, chunks - 1]
+        blocks = blocks[:-wave_count] + [seen_ids[k] for k in range(wave_count)]
+        grid = synthesize(zonal_matrix(blocks, lon_ids), whole, from_waves(rest), pieces[0], pieces, grid)
+    return grid
 
 
 def solution(mesh):

time: 711 us -> 648 us (0.911)
  starting transfers between devices: 161 us -> 27.2 us
  waiting for transfers between devices: 280 us -> 362 us
  between operations: 0.81 us -> 13.6 us
  other arithmetic: 35.6 us -> 23.9 us
  blocking collectives: 104 us -> 95.6 us
    ppermute x15 -> x3, waiting for transfers between devices: 210 us -> 0.01 us  [from_waves(): lax.ppermute(values, 'wave', [(w, (w + k) % wave_count) for w in range(wa...]
    all_gather x0 -> x4, waiting for transfers between devices: none -> 202 us  [gather_waves(): return lax.all_gather(values, 'wave', axis=0)]
    ppermute x15 -> x3, starting transfers between devices: 133 us -> 3.16 us  [from_waves(): lax.ppermute(values, 'wave', [(w, (w + k) % wave_count) for w in range(wa...]
    all_to_all x6 -> x5, waiting for transfers between devices: 69.5 us -> 159 us  [swap_lat(): lax.all_to_all(values, 'lat', split_axis=0, concat_axis=0, tiled=True)]
    another operation x2 -> x1, other arithmetic: 17.5 us -> 1.24 us
    all_to_all x2 -> x3, blocking collectives: 104 us -> 95.6 us  [swap_lat(): lax.all_to_all(values, 'lat', split_axis=0, concat_axis=0, tiled=True)]
    all_to_all x6 -> x5, starting transfers between devices: 27.6 us -> 23.5 us  [swap_lat(): lax.all_to_all(values, 'lat', split_axis=0, concat_axis=0, tiled=True)]
  transfers between devices with their start and end apart: 21 -> 12, of which waited for: 9 -> 8; matrix products, arithmetic and copies ran while one was open for 7% -> 4% of each run, Pallas kernels for 7% -> 13%
where the time goes in v3:
time: 648 us; the launch traced here: 644 us
  waiting for transfers between devices  362 us (56%)
  Pallas kernels  99 us (15%)
  blocking collectives  95.6 us (15%)
  starting transfers between devices  27.2 us (4%)
  other arithmetic  23.9 us (4%)
  local copies, waits for them, and re-layouts  22.4 us (3%)
  between operations  13.6 us (2%)
    all_gather x4, waiting for transfers between devices, gather_waves(): return lax.all_gather(values, 'wave', axis=0)  202 us
    all_to_all x5, waiting for transfers between devices, swap_lat(): lax.all_to_all(values, 'lat', split_axis=0, concat_axis=0, tiled=True)  159 us
    all_to_all x3, blocking collectives, swap_lat(): lax.all_to_all(values, 'lat', split_axis=0, concat_axis=0, tiled=True)  95.6 us
    pallas_call x2, Pallas kernels, synthesize(): pl.pallas_call(zonal_kernel if grid is None else zonal_tail_kernel, out_s...  32.3 us
    pallas_call x4, Pallas kernels, wave_step(): pl.pallas_call(wave_kernel, out_shape=jax.ShapeDtypeStruct((2, pair_count...  29.7 us
    all_to_all x5, starting transfers between devices, swap_lat(): lax.all_to_all(values, 'lat', split_axis=0, concat_axis=0, tiled=True)  23.5 us
    pallas_call x1, Pallas kernels, make_factors(): pl.pallas_call(factor_kernel, out_shape=(jax.ShapeDtypeStruct((systems, 6...  21.7 us
    pallas_call x4, Pallas kernels, pair_rows(): pl.pallas_call(pair_kernel, out_shape=[jax.ShapeDtypeStruct((piece, 2 * s...  15.3 us
  transfers between devices with their start and end apart: 12, of which 8 were waited for; matrix products, arithmetic and copies ran while one was open for 4% of the time, Pallas kernels for 13%

profile of v3, /device:TPU:0, one launch (start us, length us, event | category | flops | bytes accessed | tf_op | source)
XLA Modules:
  0.0 644.0 jit_solution(14419786509738402912)
XLA Ops:
  8.1 3.2 slice.180
  13.8 4.8 fusion.20
  25.6 5.5 all-to-all-start.1
  37.3 21.7 %factor.1 = (f32[8,6,8,100]{3,2,1,0:T(8,128)}, f32[8,6,8,128]{3,2,1,0:T(8,128)}) custom-call(f32[8,5,8,100]{3,2,1,0:T(8,128)} %copy-done.10), custom_call_target="tpu_custom_call" | custom-call | flops 2000000000 | bytes 2000000 | tf_op jit(solution)/shard_map/factor/pallas_call | solution.py:209
  62.0 17.1 %all-to-all-done.1 = bf16[8,200,1184]{2,1,0:T(8,128)(2,1)} async-done(((bf16[8,200,1184]{2,1,0:T(8,128)(2,1)}), bf16[8,200,1184]{2,1,0:T(8,128)(2,1)}, u32[]{:S(2)}, u32[]{:S(2)}) %all-to-all-start.1) | async-done | bytes 3788832 | tf_op jit(solution)/shard_map/all_to_all | solution.py:339
  79.1 7.6 %wave.5 = bf16[2,800,384]{2,1,0:T(8,128)(2,1)} custom-call(bf16[2,800,1184]{2,1,0:T(8,128)(2,1)} %bitcast.19.arrived_ref, f32[2,6,8,100]{3,2,1,0:T(8,128)} %get-tuple-element.39.factors_ref, f32[2,6,8,128]{3,2,1,0:T(8,128)} %get-tuple-element.35.links_ref), custom_call_target="tpu_custom_call" | custom-call | flops 8000000000 | bytes 6000000 | tf_op jit(solution)/shard_map/wave/pallas_call | solution.py:225
  86.7 21.5 %all_to_all.40 = bf16[8,200,384]{2,1,0:T(8,128)(2,1)} all-to-all(bf16[8,200,384]{2,1,0:T(8,128)(2,1)} %bitcast.76), channel_id=1, replica_groups=mesh['lat'=8,'wave'=4] {'lat'}, dimensions={0} | all-to-all | bytes 2457600 | tf_op jit(solution)/shard_map/all_to_all | solution.py:339
  108.3 4.5 all-to-all-start
  112.8 4.5 pad_maximum_fusion.2
  117.4 3.0 pair.4
  120.3 40.6 %all-to-all-done = bf16[8,200,1184]{2,1,0:T(8,128)(2,1)} async-done(((bf16[8,200,1184]{2,1,0:T(8,128)(2,1)}), bf16[8,200,1184]{2,1,0:T(8,128)(2,1)}, u32[]{:S(2)}, u32[]{:S(2)}) %all-to-all-start) | async-done | bytes 3788832 | tf_op jit(solution)/shard_map/all_to_all | solution.py:339
  160.9 4.5 all-to-all-start.3
  165.5 7.4 %wave.4 = bf16[2,800,384]{2,1,0:T(8,128)(2,1)} custom-call(bf16[2,800,1184]{2,1,0:T(8,128)(2,1)} %bitcast.15.arrived_ref, f32[2,6,8,100]{3,2,1,0:T(8,128)} %get-tuple-element.40.factors_ref, f32[2,6,8,128]{3,2,1,0:T(8,128)} %get-tuple-element.36.links_ref), custom_call_target="tpu_custom_call" | custom-call | flops 8000000000 | bytes 6000000 | tf_op jit(solution)/shard_map/wave/pallas_call | solution.py:225
  172.9 40.6 %all-to-all-done.3 = bf16[8,200,1184]{2,1,0:T(8,128)(2,1)} async-done(((bf16[8,200,1184]{2,1,0:T(8,128)(2,1)}), bf16[8,200,1184]{2,1,0:T(8,128)(2,1)}, u32[]{:S(2)}, u32[]{:S(2)}) %all-to-all-start.3) | async-done | bytes 3788832 | tf_op jit(solution)/shard_map/all_to_all | solution.py:339
  213.5 7.4 %wave.6 = bf16[2,800,384]{2,1,0:T(8,128)(2,1)} custom-call(bf16[2,800,1184]{2,1,0:T(8,128)(2,1)} %bitcast.22.arrived_ref, f32[2,6,8,100]{3,2,1,0:T(8,128)} %get-tuple-element.38.factors_ref, f32[2,6,8,128]{3,2,1,0:T(8,128)} %get-tuple-element.34.links_ref), custom_call_target="tpu_custom_call" | custom-call | flops 8000000000 | bytes 6000000 | tf_op jit(solution)/shard_map/wave/pallas_call | solution.py:225
  220.9 4.3 all-to-all-start.4
  225.6 3.6 pad_maximum_fusion.1
  229.2 13.3 %all-to-all-done.4 = bf16[8,200,384]{2,1,0:T(8,128)(2,1)} async-done(((bf16[8,200,384]{2,1,0:T(8,128)(2,1)}), bf16[8,200,384]{2,1,0:T(8,128)(2,1)}, u32[]{:S(2)}, u32[]{:S(2)}) %all-to-all-start.4) | async-done | bytes 1228832 | tf_op jit(solution)/shard_map/all_to_all | solution.py:339
  242.5 2.9 pair.5
  245.5 52.5 %all_to_all.41 = bf16[8,200,1184]{2,1,0:T(8,128)(2,1)} all-to-all(bf16[8,200,1184]{2,1,0:T(8,128)(2,1)} %pad_maximum_fusion.1), channel_id=1, replica_groups=mesh['lat'=8,'wave'=4] {'lat'}, dimensions={0} | all-to-all | bytes 7577600 | tf_op jit(solution)/shard_map/all_to_all | solution.py:339
  297.9 7.3 %wave.7 = bf16[2,800,384]{2,1,0:T(8,128)(2,1)} custom-call(bf16[2,800,1184]{2,1,0:T(8,128)(2,1)} %bitcast.72, f32[2,6,8,100]{3,2,1,0:T(8,128)} %get-tuple-element.37.factors_ref, f32[2,6,8,128]{3,2,1,0:T(8,128)} %get-tuple-element.33.links_ref), custom_call_target="tpu_custom_call" | custom-call | flops 8000000000 | bytes 6000000 | tf_op jit(solution)/shard_map/wave/pallas_call | solution.py:225
  305.3 21.5 %all_to_all.42 = bf16[8,200,384]{2,1,0:T(8,128)(2,1)} all-to-all(bf16[8,200,384]{2,1,0:T(8,128)(2,1)} %bitcast.77), channel_id=1, replica_groups=mesh['lat'=8,'wave'=4] {'lat'}, dimensions={0} | all-to-all | bytes 2457600 | tf_op jit(solution)/shard_map/all_to_all | solution.py:339
  326.8 2.8 pair.6
  331.0 4.6 all-to-all-start.7
  336.8 8.0 %select_convert_fusion = (bf16[800,256]{1,0:T(8,128)(2,1)}, bf16[800,256]{1,0:T(8,128)(2,1)}) fusion(s32[256]{0:T(256)S(1)} %concatenate.33, s32[800]{0:T(1024)S(1)} %iota_add_fusion, pred[256]{0:T(512)(128)(4,1)S(1)} %concatenate.26, s32[256]{0:T(256)S(1)} %concatenate.28), kind=kLoop, calls=%fused_computation.12 | loop fusion | flops 4915200 | bytes 824704 | tf_op jit(solution)/shard_map/convert_element_type | solution.py:25
  344.8 47.7 %all-to-all-done.7 = bf16[8,4,200,384]{3,2,1,0:T(8,128)(2,1)} async-done(((bf16[8,4,200,384]{3,2,1,0:T(8,128)(2,1)}), bf16[8,4,200,384]{3,2,1,0:T(8,128)(2,1)}, u32[]{:S(2)}, u32[]{:S(2)}) %all-to-all-start.7) | async-done | bytes 4915232 | tf_op jit(solution)/shard_map/all_to_all | solution.py:339
  392.5 6.6 %pair.7.refs_0_ = bf16[100,64,384]{2,1,0:T(8,128)(2,1)} custom-call(bf16[32,25,8,384]{3,2,1,0:T(8,128)(2,1)} %bitcast.28.rows_ref), custom_call_target="tpu_custom_call" | custom-call | flops 2000000000 | bytes 2400000 | tf_op jit(solution)/shard_map/pair/pallas_call | solution.py:251
  399.1 7.2 %all-gather.14.cloned.1.call-done = bf16[320,16,384]{2,1,0:T(8,128)(2,1)} async-done(((bf16[80,16,384]{2,1,0:T(8,128)(2,1)}), bf16[320,16,384]{2,1,0:T(8,128)(2,1)}) %all-gather.14.cloned.1.call-update) | async-done | bytes 3932176 | tf_op jit(solution)/shard_map/all_gather | solution.py:342
  409.5 99.4 %all-gather.10.cloned.1.call-done = bf16[400,16,384]{2,1,0:T(8,128)(2,1)} async-done(((bf16[100,16,384]{2,1,0:T(8,128)(2,1)}), bf16[400,16,384]{2,1,0:T(8,128)(2,1)}) %all-gather.10.cloned.1.call-update) | async-done | bytes 4915216 | tf_op jit(solution)/shard_map/all_gather | solution.py:342
  508.9 95.2 %all-gather.12.cloned.1.call-done = bf16[400,16,384]{2,1,0:T(8,128)(2,1)} async-done(((bf16[100,16,384]{2,1,0:T(8,128)(2,1)}), bf16[400,16,384]{2,1,0:T(8,128)(2,1)}) %all-gather.12.cloned.1.call-update) | async-done | bytes 4915216 | tf_op jit(solution)/shard_map/all_gather | solution.py:342
  604.1 24.3 %zonal.2.refs_7_ = bf16[800,38400]{1,0:T(8,128)(2,1)} custom-call(bf16[800,256]{1,0:T(8,128)(2,1)} %get-tuple-element.53.trig_ref, bf16[100,64,384]{2,1,0:T(8,128)(2,1)} %pair.7.refs_0_, bf16[4,100,16,384]{3,2,1,0:T(8,128)(2,1)} %bitcast.68, bf16[4,100,16,384]{3,2,1,0:T(8,128)(2,1)} %bitcast.70, bf16[4,80,16,384]{3,2,1,0:T(8,128)(2,1)} %bitcast.80), custom_call_target="tpu_custom_call" | custom-call | flops 25165824000 | bytes 49152000 | tf_op jit(solution)/shard_map/zonal/pallas_call | solution.py:281
  629.3 8.1 %zonal.3 = bf16[800,38400]{1,0:T(8,128)(2,1)} custom-call(bf16[800,256]{1,0:T(8,128)(2,1)} %get-tuple-element.54.trig_ref, bf16[100,64,384]{2,1,0:T(8,128)(2,1)} %pair.7.refs_0_, bf16[4,100,16,384]{3,2,1,0:T(8,128)(2,1)} %bitcast.69, bf16[4,100,16,384]{3,2,1,0:T(8,128)(2,1)} %bitcast.71, ...), custom_call_target="tpu_custom_call", output_to_operand_aliasing={{}: (8, {})} | custom-call | flops 6291456000 | bytes 12288000 | tf_op jit(solution)/shard_map/zonal/pallas_call | solution.py:281
  (83 shorter events, 27.2 us)
Async XLA Ops:
  6.5 13.5 %copy-start = (f32[32,200,800]{2,1,0:T(8,128)S(1)}, f32[32,200,800]{2,1,0:T(8,128)}, u32[]{:S(2)}) copy-start(f32[32,200,800]{2,1,0:T(8,128)} %param.7) | copy-start | bytes 61440004
  21.3 2.0 copy-start.1
  25.6 6.1 copy-start.11
  25.6 6.9 %copy-start.6 = (f32[32,1600]{1,0:T(8,128)S(1)}, f32[32,1600]{1,0:T(8,128)}, u32[]{:S(2)}) copy-start(f32[32,1600]{1,0:T(8,128)} %param.9) | copy-start | bytes 614404
  25.6 7.8 %copy-start.7 = (f32[32,1600]{1,0:T(8,128)S(1)}, f32[32,1600]{1,0:T(8,128)}, u32[]{:S(2)}) copy-start(f32[32,1600]{1,0:T(8,128)} %param.10) | copy-start | bytes 614404
  25.6 53.5 %all-to-all-start.1 = ((bf16[8,200,1184]{2,1,0:T(8,128)(2,1)}), bf16[8,200,1184]{2,1,0:T(8,128)(2,1)}, u32[]{:S(2)}, u32[]{:S(2)}) async-start(bf16[8,200,1184]{2,1,0:T(8,128)(2,1)} %pad_maximum_fusion.3), calls=%async_computation.1 | async-start | bytes 8192000 | tf_op jit(solution)/shard_map/all_to_all | solution.py:339
  31.8 0.6 copy-start.8
  36.6 0.7 copy-start.10
  108.3 52.6 %all-to-all-start = ((bf16[8,200,1184]{2,1,0:T(8,128)(2,1)}), bf16[8,200,1184]{2,1,0:T(8,128)(2,1)}, u32[]{:S(2)}, u32[]{:S(2)}) async-start(bf16[8,200,1184]{2,1,0:T(8,128)(2,1)} %pad_maximum_fusion), calls=%async_computation | async-start | bytes 8192000 | tf_op jit(solution)/shard_map/all_to_all | solution.py:339
  160.9 52.6 %all-to-all-start.3 = ((bf16[8,200,1184]{2,1,0:T(8,128)(2,1)}), bf16[8,200,1184]{2,1,0:T(8,128)(2,1)}, u32[]{:S(2)}, u32[]{:S(2)}) async-start(bf16[8,200,1184]{2,1,0:T(8,128)(2,1)} %pad_maximum_fusion.2), calls=%async_computation.3 | async-start | bytes 8192000 | tf_op jit(solution)/shard_map/all_to_all | solution.py:339
  165.4 165.5 %all-gather.8.cloned.1.call-start = ((), (), s32[]{:S(2)}) async-start(), calls=%async_computation.8 | async-start | bytes 6144000 | tf_op jit(solution)/shard_map/all_gather | solution.py:342
  220.9 21.6 %all-to-all-start.4 = ((bf16[8,200,384]{2,1,0:T(8,128)(2,1)}), bf16[8,200,384]{2,1,0:T(8,128)(2,1)}, u32[]{:S(2)}, u32[]{:S(2)}) async-start(bf16[8,200,384]{2,1,0:T(8,128)(2,1)} %bitcast.74), calls=%async_computation.4 | async-start | bytes 2457600 | tf_op jit(solution)/shard_map/all_to_all | solution.py:339
  225.2 181.2 %all-gather.14.cloned.1.call-start = ((), (), s32[]{:S(2)}) async-start(), calls=%async_computation.11 | async-start | bytes 4915200 | tf_op jit(solution)/shard_map/all_gather | solution.py:342
  329.6 179.3 %all-gather.10.cloned.1.call-start = ((), (), s32[]{:S(2)}) async-start(), calls=%async_computation.9 | async-start | bytes 6144000 | tf_op jit(solution)/shard_map/all_gather | solution.py:342
  330.4 273.7 %all-gather.12.cloned.1.call-start = ((), (), s32[]{:S(2)}) async-start(), calls=%async_computation.10 | async-start | bytes 6144000 | tf_op jit(solution)/shard_map/all_gather | solution.py:342
  331.0 4.7 copy-start.9
  331.0 5.3 slice-start
  331.0 61.5 %all-to-all-start.7 = ((bf16[8,4,200,384]{3,2,1,0:T(8,128)(2,1)}), bf16[8,4,200,384]{3,2,1,0:T(8,128)(2,1)}, u32[]{:S(2)}, u32[]{:S(2)}) async-start(bf16[8,4,200,384]{3,2,1,0:T(8,128)(2,1)} %bitcast.67), calls=%async_computation.7 | async-start | bytes 9830400 | tf_op jit(solution)/shard_map/all_to_all | solution.py:339
  392.5 13.8 %copy-start.2 = (bf16[20,16,384]{2,1,0:T(8,128)(2,1)S(1)}, bf16[20,16,384]{2,1,0:T(8,128)(2,1)}, u32[]{:S(2)}) copy-start(bf16[20,16,384]{2,1,0:T(8,128)(2,1)} %get-tuple-element.24.refs_3_) | copy-start | bytes 737284
  406.4 222.0 %collective-permute-start.2 = (bf16[20,16,384]{2,1,0:T(8,128)(2,1)S(1)}, bf16[20,16,384]{2,1,0:T(8,128)(2,1)S(1)}, u32[]{:S(2)}, u32[]{:S(2)}) collective-permute-start(bf16[20,16,384]{2,1,0:T(8,128)(2,1)S(1)} %copy-done.2), channel_id=1, source_target_pairs={{0,3},{1,0},{2,1},{3,2},{4,7},{5,4},{6,5},{7,6},{8,11},{9,8},{10,9... | collective-permute-start | bytes 737288 | tf_op jit(solution)/shard_map/ppermute | solution.py:346
  407.0 221.4 %collective-permute-start.1 = (bf16[20,16,384]{2,1,0:T(8,128)(2,1)S(1)}, bf16[20,16,384]{2,1,0:T(8,128)(2,1)S(1)}, u32[]{:S(2)}, u32[]{:S(2)}) collective-permute-start(bf16[20,16,384]{2,1,0:T(8,128)(2,1)S(1)} %copy-done.2), channel_id=1, source_target_pairs={{0,2},{1,3},{2,0},{3,1},{4,6},{5,7},{6,4},{7,5},{8,10},{9,11},{10,... | collective-permute-start | bytes 737288 | tf_op jit(solution)/shard_map/ppermute | solution.py:346
  407.3 221.1 %collective-permute-start = (bf16[20,16,384]{2,1,0:T(8,128)(2,1)S(1)}, bf16[20,16,384]{2,1,0:T(8,128)(2,1)S(1)}, u32[]{:S(2)}, u32[]{:S(2)}) collective-permute-start(bf16[20,16,384]{2,1,0:T(8,128)(2,1)S(1)} %copy-done.2), channel_id=1, source_target_pairs={{0,1},{1,2},{2,3},{3,0},{4,5},{5,6},{6,7},{7,4},{8,9},{9,10},{10,1... | collective-permute-start | bytes 737288 | tf_op jit(solution)/shard_map/ppermute | solution.py:346
  628.4 0.7 copy-start.3
  628.4 0.8 copy-start.4
  628.4 0.9 copy-start.5
Sparse Core Ops, SparseCore 0:
  173.0 94.9 all-gather.7
  329.8 76.5 all-gather.13
  407.9 100.9 all-gather.9
  510.3 93.7 all-gather.11
